TPU v7x, 512 devices: a whole 4x8x8 slice. The times are simulated.
512 devices in a mesh: tf: 128 (over y_hi, x, z), inp: 4 (over y_lo, core).
Axes of the slice: x: 4, y: 8 (y_hi: 4, y_lo: 2; y = y_hi * 2 + y_lo), z: 8, core: 2. Of those that a mesh axis runs over, the one named last changes fastest.
Arguments:
- voltages: bfloat16 [384, 2048, 1024], P('tf', None, 'inp'), may hold values from -6 to 6
- channel_gain: float32 [128, 1024], P(None, 'inp'), may hold values from 0.5 to 1.5
Outputs:
- visibility: float32 [128, 1024, 1024], P('tf', 'inp')
All inputs are finite; a program needn't handle non-finite values.
Results may differ from a plain program's by a relative error of at most 0.0042.
Values may be sent and summed in bfloat16 or wider, within the bound.
No kernel may reach another device: no remote copies, remote signals or barrier semaphores. Data moves between devices by JAX's collectives and lax.ppermute only.
A program may use at most 64 MiB of HBM per device.

v0:
```python
import math

import jax
import jax.numpy as jnp
from jax import lax
from jax.sharding import PartitionSpec as P

TAPS = 4


def passed_along(block, axis, distance):
    devices = range(lax.axis_size(axis))
    route = [(i - distance, i) for i in devices if i - distance in devices]
    return lax.ppermute(block, axis, route)


def build_table(frame_len, channels, taps):
    length = taps * frame_len
    sample = jnp.arange(length).astype(jnp.float32)
    window = jnp.sinc((sample - length / 2 + 0.5) / frame_len) * (
        0.5 - 0.5 * jnp.cos(2.0 * math.pi * (sample + 0.5) / length)
    )
    first_channel = (frame_len // 2 - channels) // 2
    phase_index = (
        jnp.arange(frame_len, dtype=jnp.int32)[:, None]
        * (first_channel + jnp.arange(channels, dtype=jnp.int32))[None, :]
        % frame_len
    )
    phase_angle = phase_index.astype(jnp.float32) * (2.0 * math.pi / frame_len)
    basis_cols = jnp.concatenate([jnp.cos(phase_angle), -jnp.sin(phase_angle)], axis=1)
    weighted = window.reshape(taps, frame_len)[:, :, None] * basis_cols[None]
    return (weighted / jnp.sqrt(jnp.sum(window * window))).astype(jnp.bfloat16)


def tail_terms(tail_block, tap_table):
    tail_count = tail_block.shape[0]
    products = []
    for tap in range(tail_count):
        product = jnp.einsum(
            "sna,nc->sca", tail_block[tap:], tap_table[tap], preferred_element_type=jnp.float32
        )
        products.append(jnp.pad(product, ((0, tap), (0, 0), (0, 0))))
    return sum(products[1:], products[0])


def correlate(own_rows, col_block, row_first, norm_scale):
    real_rows = own_rows[:, 0, 0]
    imag_rows = own_rows[:, 1, 0]
    real_cols = col_block[:, 0, 0]
    imag_cols = col_block[:, 1, 0]
    real_sum = jnp.einsum(
        "tka,tkw->kaw", real_rows, real_cols, preferred_element_type=jnp.float32
    ) + jnp.einsum("tka,tkw->kaw", imag_rows, imag_cols, preferred_element_type=jnp.float32)
    imag_sum = jnp.einsum(
        "tka,tkw->kaw", imag_rows, real_cols, preferred_element_type=jnp.float32
    ) - jnp.einsum("tka,tkw->kaw", real_rows, imag_cols, preferred_element_type=jnp.float32)
    row_index = row_first + jnp.arange(own_rows.shape[4], dtype=jnp.int32)
    col_index = jnp.arange(col_block.shape[4], dtype=jnp.int32)
    upper_half = row_index[:, None] <= col_index[None, :]
    return jnp.where(upper_half[None], real_sum, imag_sum) * norm_scale


def shards(voltages, channel_gain):
    steps_dev = voltages.shape[0]
    frame_len = voltages.shape[1]
    block_width = voltages.shape[2]
    channels = channel_gain.shape[0]
    tap_table = build_table(frame_len, channels, TAPS)
    lead_frames = TAPS - 1
    local_parts = []
    for tap in range(TAPS):
        lead = lead_frames - tap
        product = jnp.einsum(
            "sna,nc->sca",
            voltages[: steps_dev - lead],
            tap_table[tap],
            preferred_element_type=jnp.float32,
        )
        local_parts.append(jnp.pad(product, ((lead, 0), (0, 0), (0, 0))))
    local_sum = sum(local_parts[1:], local_parts[0])
    earlier = passed_along(voltages, "tf", 1)
    carried = tail_terms(earlier, tap_table)
    summed = local_sum + jnp.pad(carried, ((0, steps_dev - lead_frames), (0, 0), (0, 0)))
    spectra = (
        summed.reshape(steps_dev, 2, channels, block_width) * channel_gain[None, None]
    ).astype(jnp.bfloat16)
    groups = lax.axis_size("tf")
    spectra = spectra.reshape(steps_dev, 2, groups, channels // groups, block_width)
    norm_scale = 1.0 / math.sqrt(steps_dev * groups)
    turned = lax.all_to_all(spectra, "tf", split_axis=2, concat_axis=0, tiled=True)
    own_first = lax.axis_index("inp") * turned.shape[4]
    return correlate(
        turned, lax.all_gather(turned, "inp", axis=4, tiled=True), own_first, norm_scale
    )


def solution(mesh):
    placed = (P("tf", None, "inp"), P(None, "inp"))
    return jax.shard_map(
        shards, mesh=mesh, in_specs=placed, out_specs=P("tf", "inp", None), check_vma=False
    )
```

profile of v0, /device:TPU:1, one launch (start us, length us, event | category | flops | bytes accessed | tf_op | source)
XLA Modules:
  0.0 228.9 jit_solution(17991282589854411832)
XLA Ops:
  6.5 0.0 all-gather.2.cloned.1.call-start
  6.5 5.0 %collective-permute-start = (bf16[3,2048,256]{2,1,0:T(8,128)(2,1)}, bf16[3,2048,256]{2,1,0:T(8,128)(2,1)S(1)}, u32[]{:S(2)}, u32[]{:S(2)}) collective-permute-start(bf16[3,2048,256]{2,1,0:T(8,128)(2,1)} %param.2), channel_id=1, source_target_pairs={{0,4},{4,8},{8,12},{12,16},{16,20},{20,24},{24,28},{28,32},{32,36}... | collective-permute-start | bytes 9437192 | tf_op jit(solution)/shard_map/ppermute | solution.py:14
  11.6 0.8 fusion.72
  13.0 0.3 fusion.66
  13.4 4.2 %fusion.39 = (f32[2048,128]{0,1:T(8,128)S(1)}, f32[2048,128]{0,1:T(8,128)S(1)}) fusion(s32[128]{0:T(128)S(1)} %iota_add_fusion.1), kind=kLoop, calls=%fused_computation.52 | loop fusion | flops 3932160 | bytes 2097664 | tf_op jit(solution)/shard_map/cos | solution.py:30
  17.5 0.1 pad_maximum_fusion
  17.7 0.0 copy-start.1
  17.7 1.1 divide_convert_fusion
  18.7 0.8 copy-done.1
  19.6 0.4 convolution_bitcast_fusion.3
  20.0 0.7 fusion.11
  20.7 1.0 fusion.7
  21.7 54.3 %collective-permute-done = bf16[3,2048,256]{2,1,0:T(8,128)(2,1)S(1)} collective-permute-done((bf16[3,2048,256]{2,1,0:T(8,128)(2,1)}, bf16[3,2048,256]{2,1,0:T(8,128)(2,1)S(1)}, u32[]{:S(2)}, u32[]{:S(2)}) %collective-permute-start) | collective-permute-done | bytes 3145760 | tf_op jit(solution)/shard_map/ppermute | solution.py:14
  76.0 0.7 fusion.14
  76.7 0.5 convolution_bitcast_fusion.2
  77.2 0.0 copy-start
  77.2 1.0 fusion.10
  78.2 0.0 copy-done
  78.2 0.1 multiply_convert_fusion
  78.3 0.4 copy.5
  78.7 39.1 %all_to_all.18 = bf16[3,2,128,1,256]{4,1,0,3,2:T(2,128)(2,1)} all-to-all(bf16[3,2,128,1,256]{4,1,0,3,2:T(2,128)(2,1)S(1)} %copy.5), channel_id=1, replica_groups=mesh['tf'=128,'inp'=4] {'tf'}, dimensions={2} | all-to-all | bytes 786432 | tf_op jit(solution)/shard_map/all_to_all | solution.py:90
  117.8 0.0 all-gather.2.cloned.1.call-update
  117.9 1.9 fusion.79
  119.7 94.8 %all-gather.2.cloned.1.call-done = bf16[384,2,1,1,1024]{4,1,0,3,2:T(2,128)(2,1)} async-done(((bf16[384,2,1,1,256]{4,1,0,3,2:T(2,128)(2,1)}), bf16[384,2,1,1,1024]{4,1,0,3,2:T(2,128)(2,1)}) %all-gather.2.cloned.1.call-update) | async-done | bytes 1572880 | tf_op jit(solution)/shard_map/all_gather | solution.py:93
  214.5 4.5 %fusion.78 = (bf16[384,1,1,1,1024]{4,1,0,3,2:T(2,128)(2,1)S(1)}, bf16[384,1,1,1,1024]{4,1,0,3,2:T(2,128)(2,1)S(1)}) fusion(bf16[384,2,1,1,1024]{4,1,0,3,2:T(2,128)(2,1)} %all-gather.2.cloned.1.call-done), kind=kLoop, calls=%fused_computation.116 | loop fusion | bytes 3145728 | tf_op jit(solution)/shard_map/slice | solution.py:50
  219.0 0.5 fusion.37
  219.5 0.5 fusion.35
  220.0 0.5 convolution_subtract_fusion
  220.5 1.5 fusion.6
  (2 shorter events, 0.0 us)
Async XLA Ops:
  6.5 208.0 %all-gather.2.cloned.1.call-start = ((), (), s32[]{:S(2)}) async-start(), calls=%async_computation.1 | async-start | bytes 1966080 | tf_op jit(solution)/shard_map/all_gather | solution.py:93
  6.5 69.4 %collective-permute-start = (bf16[3,2048,256]{2,1,0:T(8,128)(2,1)}, bf16[3,2048,256]{2,1,0:T(8,128)(2,1)S(1)}, u32[]{:S(2)}, u32[]{:S(2)}) collective-permute-start(bf16[3,2048,256]{2,1,0:T(8,128)(2,1)} %param.2), channel_id=1, source_target_pairs={{0,4},{4,8},{8,12},{12,16},{16,20},{20,24},{24,28},{28,32},{32,36}... | collective-permute-start | bytes 9437192 | tf_op jit(solution)/shard_map/ppermute | solution.py:14
  17.7 1.9 copy-start.1
  77.2 1.0 copy-start
Sparse Core Ops, SparseCore 0:
  118.0 96.4 all-gather.1
where the time goes:
time: 229 us
  waiting for transfers between devices  149 us (65%)
  blocking collectives  39.1 us (17%)
  between operations  14.2 us (6%)
  local copies, waits for them, and re-layouts  7.57 us (3%)
  matrix products  7.31 us (3%)
  other arithmetic  6.54 us (3%)
  starting transfers between devices  5.02 us (2%)
    all_gather x1, waiting for transfers between devices, shards(): lax.all_gather(turned, 'inp', axis=4, tiled=True)  94.8 us
    ppermute x1, waiting for transfers between devices, passed_along(): return lax.ppermute(block, axis, route)  54.3 us
    all_to_all x1, blocking collectives, shards(): lax.all_to_all(spectra, 'tf', split_axis=2, concat_axis=0, tiled=True)  39.1 us
    ppermute x1, starting transfers between devices, passed_along(): return lax.ppermute(block, axis, route)  5.02 us
  transfers between devices with their start and end apart: 2, of which 2 were waited for; matrix products, arithmetic and copies ran while one was open for 5% of the time, Pallas kernels for 0%

commit v1 on v0

v1 whole, which is shorter than its diff:
```python
import functools
import math

import jax
import jax.numpy as jnp
from jax import lax
from jax.experimental import pallas as pl
from jax.experimental.pallas import tpu as pltpu
from jax.sharding import PartitionSpec as P

TAPS = 4
LANES = 128


def tap_window(frame_len):
    length = TAPS * frame_len
    shape = (length // LANES, LANES)
    sample = (
        lax.broadcasted_iota(jnp.int32, shape, 0) * LANES
        + lax.broadcasted_iota(jnp.int32, shape, 1)
    ).astype(jnp.float32)
    angle = math.pi * ((sample - length / 2 + 0.5) / frame_len)
    window = jnp.sin(angle) / angle * (
        0.5 - 0.5 * jnp.cos(2.0 * math.pi * (sample + 0.5) / length)
    )
    return window / jnp.sqrt(jnp.sum(window * window))


def fill_table(window_ref, table_ref, frame_len, channels):
    window_ref[...] = tap_window(frame_len)
    first_channel = (frame_len // 2 - channels) // 2
    rows = frame_len // LANES
    step = 2.0 * math.pi / frame_len
    channel = first_channel + lax.broadcasted_iota(jnp.int32, (channels, LANES), 0)
    lane = lax.broadcasted_iota(jnp.int32, (channels, LANES), 1)
    low = (channel * lane % frame_len).astype(jnp.float32) * step
    cos_low, sin_low = jnp.cos(low), jnp.sin(low)
    few = lax.broadcasted_iota(jnp.int32, (rows, LANES), 0) + first_channel
    part = lax.broadcasted_iota(jnp.int32, (rows, LANES), 1)
    high = (few * part % rows).astype(jnp.float32) * (2.0 * math.pi / rows)
    cos_high, sin_high = jnp.cos(high), jnp.sin(high)
    repeats = channels // rows

    def spread(values, h):
        column = jnp.broadcast_to(values[:, h : h + 1], (rows, LANES))
        return jnp.broadcast_to(column[None], (repeats, rows, LANES)).reshape(channels, LANES)

    for h in range(rows):
        cos_h, sin_h = spread(cos_high, h), spread(sin_high, h)
        cos_all = cos_low * cos_h - sin_low * sin_h
        sin_all = -(sin_low * cos_h + cos_low * sin_h)
        for k in range(TAPS):
            weight = window_ref[k * rows + h : k * rows + h + 1, :]
            at = slice(h * LANES, (h + 1) * LANES)
            table_ref[k, :channels, at] = (cos_all * weight).astype(jnp.bfloat16)
            table_ref[k, channels:, at] = (sin_all * weight).astype(jnp.bfloat16)


def partial_kernel(volts, kept, ahead, back, frames, table, window, sems):
    count, frame_len, width = frames.shape
    copies = [pltpu.make_async_copy(volts.at[f], frames.at[f], sems.at[f]) for f in range(count)]
    for copy in copies:
        copy.start()
    fill_table(window, table, frame_len, table.shape[1] // 2)
    for copy in copies:
        copy.wait()

    def spectrum(s):
        total = None
        for f in range(count):
            k = f + TAPS - 1 - s
            if 0 <= k < TAPS:
                product = jnp.dot(table[k], frames[f], preferred_element_type=jnp.float32)
                total = product if total is None else total + product
        return total

    ahead[0] = spectrum(4)
    ahead[1] = spectrum(5)
    back[0] = spectrum(0)
    for at, s in enumerate((1, 2, 3)):
        kept[at] = spectrum(s)


def partial_spectra(voltages, channels):
    count, frame_len, width = voltages.shape
    out = lambda n: jax.ShapeDtypeStruct((n, 2 * channels, width), jnp.float32)
    return pl.pallas_call(
        partial_kernel,
        out_shape=(out(3), out(2), out(1)),
        in_specs=[pl.BlockSpec(memory_space=pl.ANY)],
        out_specs=[pl.BlockSpec(memory_space=pltpu.VMEM)] * 3,
        scratch_shapes=[
            pltpu.VMEM((count, frame_len, width), jnp.bfloat16),
            pltpu.VMEM((TAPS, 2 * channels, frame_len), jnp.bfloat16),
            pltpu.VMEM((TAPS * frame_len // LANES, LANES), jnp.float32),
            pltpu.SemaphoreType.DMA((count,)),
        ],
        compiler_params=pltpu.CompilerParams(vmem_limit_bytes=32 * 1024 * 1024),
        cost_estimate=pl.CostEstimate(
            flops=2 * 12 * 2 * channels * frame_len * width,
            bytes_accessed=voltages.size * 2 + 6 * 2 * channels * width * 4,
            transcendentals=0,
        ),
    )(voltages)


def visibility_kernel(norm_scale, place, own, side, far, far_side, out, turned):
    rows, width = own.shape
    mine = place[0]
    plain = own[...].astype(jnp.float32)
    even = lax.broadcasted_iota(jnp.int32, (rows, width), 0) % 2 == 0
    turned[0] = own[...]
    turned[1] = jnp.where(even, jnp.roll(plain, -1, 0), -jnp.roll(plain, 1, 0)).astype(jnp.bfloat16)
    contract = (((0,), (0,)), ((), ()))

    def product(left, right):
        return lax.dot_general(left, right, contract, preferred_element_type=jnp.float32)

    def place_block(other, value):
        out[0, :, pl.ds(pl.multiple_of(other * width, width), width)] = value * norm_scale

    upper = lax.broadcasted_iota(jnp.int32, (width, width), 0) <= lax.broadcasted_iota(
        jnp.int32, (width, width), 1
    )
    place_block(
        mine, jnp.where(upper, product(turned[0], own[...]), product(turned[1], own[...]))
    )
    for flip, block in ((1, side), (2, far), (3, far_side)):
        other = mine ^ flip
        place_block(other, product(turned[(other < mine).astype(jnp.int32)], block[...]))


def visibilities(place, blocks, norm_scale):
    rows, width = blocks[0].shape
    return pl.pallas_call(
        functools.partial(visibility_kernel, norm_scale),
        out_shape=jax.ShapeDtypeStruct((1, width, 4 * width), jnp.float32),
        in_specs=[pl.BlockSpec(memory_space=pltpu.SMEM)]
        + [pl.BlockSpec(memory_space=pltpu.VMEM)] * 4,
        out_specs=pl.BlockSpec(memory_space=pltpu.VMEM),
        scratch_shapes=[pltpu.VMEM((2, rows, width), jnp.bfloat16)],
        compiler_params=pltpu.CompilerParams(vmem_limit_bytes=32 * 1024 * 1024),
        cost_estimate=pl.CostEstimate(
            flops=2 * 5 * rows * width * width,
            bytes_accessed=4 * rows * width * 2 + 4 * width * width * 4,
            transcendentals=0,
        ),
    )(place, *blocks)


def shards(voltages, channel_gain):
    channels, width = channel_gain.shape
    groups = lax.axis_size("tf")
    own_group = lax.axis_index("tf")
    kept, ahead, back = partial_spectra(voltages, channels)
    from_before = lax.ppermute(ahead, "tf", [(i, i + 1) for i in range(groups - 1)])
    from_after = lax.ppermute(back, "tf", [(i, (i - 1) % groups) for i in range(groups)])
    third = jnp.where(own_group == groups - 1, 0.0, kept[2:]) + from_after
    summed = jnp.concatenate([kept[:2] + from_before, third], axis=0)
    spectra = (
        summed.reshape(3, 2, channels, width) * channel_gain[None, None]
    ).astype(jnp.bfloat16)
    spectra = spectra.transpose(2, 0, 1, 3)
    turned = lax.all_to_all(spectra, "tf", split_axis=0, concat_axis=0, tiled=True)
    own = turned.reshape(groups * 6, width)
    far = lax.ppermute(own, "inp", [(i, i ^ 2) for i in range(4)])
    side = lax.ppermute(own, "inp", [(i, i ^ 1) for i in range(4)])
    far_side = lax.ppermute(far, "inp", [(i, i ^ 1) for i in range(4)])
    place = lax.axis_index("inp").astype(jnp.int32).reshape(1)
    norm_scale = 1.0 / math.sqrt(3 * groups)
    return visibilities(place, (own, side, far, far_side), norm_scale)


def solution(mesh):
    placed = (P("tf", None, "inp"), P(None, "inp"))
    return jax.shard_map(
        shards, mesh=mesh, in_specs=placed, out_specs=P("tf", "inp", None), check_vma=False
    )
```

time: 229 us -> 88.5 us (0.39)
  waiting for transfers between devices: 149 us -> 13.8 us
  starting transfers between devices: 5.02 us -> 36.4 us
  between operations: 14.2 us -> 0.13 us
  blocking collectives: 39.1 us -> 27.8 us
  Pallas kernels: 0 us -> 7.44 us
  matrix products: 7.31 us -> 0 us
  other arithmetic: 6.54 us -> 0.24 us
  local copies, waits for them, and re-layouts: 7.57 us -> 2.45 us
    all_gather x1 -> x0, waiting for transfers between devices: 94.8 us -> none  [shards(): lax.all_gather(turned, 'inp', axis=4, tiled=True)]
    ppermute x1 -> x5, waiting for transfers between devices: 54.3 us -> 13.8 us  [the longest x1 11.4 us: shards(): lax.ppermute(back, 'tf', [(i, (i - 1) % groups) for i in range(groups)])]
    ppermute x1 -> x5, starting transfers between devices: 5.02 us -> 36.4 us  [the longest x1 13.8 us: shards(): lax.ppermute(back, 'tf', [(i, (i - 1) % groups) for i in range(groups)])]
    all_to_all x1, blocking collectives: 39.1 us -> 27.8 us  [shards(): lax.all_to_all(spectra, 'tf', split_axis=0, concat_axis=0, tiled=True)]
    pallas_call x0 -> x2, Pallas kernels: none -> 7.44 us  [the longest x1 5.6 us: partial_spectra(): pl.pallas_call(partial_kernel, out_shape=(out(3), out(2), out(1)), in_spe...]
    dot_general x10 -> x0, matrix products: 7.31 us -> none  [the longest x3 2.2 us: tail_terms(): jnp.einsum('sna,nc->sca', tail_block[tap:], tap_table[tap], preferred_ele...]
    slice x2 -> x0, local copies, waits for them, and re-layouts: 6.33 us -> none  [the longest x1 4.48 us: correlate(): imag_cols = col_block[:, 1, 0]]
    cos x1 -> x0, other arithmetic: 4.16 us -> none  [build_table(): jnp.cos(phase_angle)]
  transfers between devices with their start and end apart: 2 -> 5, of which waited for: 2 -> 3; matrix products, arithmetic and copies ran while one was open for 5% -> 0% of each run, Pallas kernels for 0% -> 0%
where the time goes in v1:
time: 88.5 us; the launch traced here: 88.2 us
  starting transfers between devices  36.4 us (41%)
  blocking collectives  27.8 us (31%)
  waiting for transfers between devices  13.8 us (16%)
  Pallas kernels  7.44 us (8%)
  local copies, waits for them, and re-layouts  2.45 us (3%)
    all_to_all x1, blocking collectives, shards(): lax.all_to_all(spectra, 'tf', split_axis=0, concat_axis=0, tiled=True)  27.8 us
    ppermute x1, starting transfers between devices, shards(): lax.ppermute(back, 'tf', [(i, (i - 1) % groups) for i in range(groups)])  13.8 us
    ppermute x1, waiting for transfers between devices, shards(): lax.ppermute(back, 'tf', [(i, (i - 1) % groups) for i in range(groups)])  11.4 us
    ppermute x1, starting transfers between devices, shards(): far = lax.ppermute(own, 'inp', [(i, i ^ 2) for i in range(4)])  6.74 us
    pallas_call x1, Pallas kernels, partial_spectra(): pl.pallas_call(partial_kernel, out_shape=(out(3), out(2), out(1)), in_spe...  5.6 us
    ppermute x1, starting transfers between devices, shards(): far_side = lax.ppermute(far, 'inp', [(i, i ^ 1) for i in range(4)])  5.59 us
    ppermute x1, starting transfers between devices, shards(): side = lax.ppermute(own, 'inp', [(i, i ^ 1) for i in range(4)])  5.24 us
    ppermute x1, starting transfers between devices, shards(): lax.ppermute(ahead, 'tf', [(i, i + 1) for i in range(groups - 1)])  4.99 us
  transfers between devices with their start and end apart: 5, of which 3 were waited for; matrix products, arithmetic and copies ran while one was open for 0% of the time, Pallas kernels for 0%

profile of v1, /device:TPU:1, one launch (start us, length us, event | category | flops | bytes accessed | tf_op | source)
XLA Modules:
  0.0 88.2 jit_solution(5516291861393448207)
XLA Ops:
  0.0 0.0 copy-start
  0.0 1.9 %copy-done = bf16[3,2048,256]{2,1,0:T(8,128)(2,1)S(1)} copy-done((bf16[3,2048,256]{2,1,0:T(8,128)(2,1)S(1)}, bf16[3,2048,256]{2,1,0:T(8,128)(2,1)}, u32[]{:S(2)}) %copy-start) | copy-done | bytes 3145752
  1.9 5.6 %shard_map.28 = (f32[3,256,256]{2,1,0:T(8,128)S(1)}, f32[2,256,256]{2,1,0:T(8,128)S(1)}, f32[1,256,256]{2,1,0:T(8,128)S(1)}) custom-call(bf16[3,2048,256]{2,1,0:T(8,128)(2,1)S(1)} %copy-done), custom_call_target="tpu_custom_call" | custom-call | flops 3221225472 | bytes 4718592 | tf_op jit(solution)/shard_map/pallas_call | solution.py:87
  7.5 0.0 copy-start.1
  7.5 5.0 %collective-permute-start = (f32[2,256,256]{2,1,0:T(8,128)S(1)}, f32[2,256,256]{2,1,0:T(8,128)S(1)}, u32[]{:S(2)}, u32[]{:S(2)}) collective-permute-start(f32[2,256,256]{2,1,0:T(8,128)S(1)} %get-tuple-element.9), channel_id=1, source_target_pairs={{0,4},{4,8},{8,12},{12,16},{16,20},{20,24},{24,28},{28,32},{32,36}... | collective-permute-start | bytes 1572872 | tf_op jit(solution)/shard_map/ppermute | solution.py:156
  12.5 13.8 %collective-permute-start.1 = (f32[1,256,256]{2,1,0:T(8,128)S(1)}, f32[1,256,256]{2,1,0:T(8,128)S(1)}, u32[]{:S(2)}, u32[]{:S(2)}) collective-permute-start(f32[1,256,256]{2,1,0:T(8,128)S(1)} %get-tuple-element.10), channel_id=1, source_target_pairs={{0,508},{4,0},{8,4},{12,8},{16,12},{20,16},{24,20},{28,24},{32,28}... | collective-permute-start | bytes 786440 | tf_op jit(solution)/shard_map/ppermute | solution.py:157
  26.3 11.4 %collective-permute-done.1 = f32[1,256,256]{2,1,0:T(8,128)S(1)} collective-permute-done((f32[1,256,256]{2,1,0:T(8,128)S(1)}, f32[1,256,256]{2,1,0:T(8,128)S(1)}, u32[]{:S(2)}, u32[]{:S(2)}) %collective-permute-start.1) | collective-permute-done | bytes 262176 | tf_op jit(solution)/shard_map/ppermute | solution.py:157
  37.7 0.0 collective-permute-done
  37.8 0.1 slice_add_fusion
  37.8 0.1 pad_maximum_fusion
  37.9 0.0 copy-done.1
  37.9 0.1 fusion
  38.0 0.4 copy.5
  38.4 27.8 %all_to_all.5 = bf16[128,3,2,256]{3,2,1,0:T(2,128)(2,1)S(1)} all-to-all(bf16[128,3,2,256]{3,2,1,0:T(2,128)(2,1)S(1)} %copy.5), channel_id=1, replica_groups=mesh['tf'=128,'inp'=4] {'tf'}, dimensions={0} | all-to-all | bytes 786432 | tf_op jit(solution)/shard_map/all_to_all | solution.py:164
  66.2 0.2 reshape.12.own
  66.3 6.7 %collective-permute-start.3 = (bf16[768,256]{1,0:T(8,128)(2,1)S(1)}, bf16[768,256]{1,0:T(8,128)(2,1)S(1)}, u32[]{:S(2)}, u32[]{:S(2)}) collective-permute-start(bf16[768,256]{1,0:T(8,128)(2,1)S(1)} %reshape.12.own), channel_id=1, source_target_pairs={{0,2},{1,3},{2,0},{3,1},{4,6},{5,7},{6,4},{7,5},{8,10},{9,11},{10,... | collective-permute-start | bytes 1179656 | tf_op jit(solution)/shard_map/ppermute | solution.py:166
  73.1 5.2 %collective-permute-start.2 = (bf16[768,256]{1,0:T(8,128)(2,1)S(1)}, bf16[768,256]{1,0:T(8,128)(2,1)S(1)}, u32[]{:S(2)}, u32[]{:S(2)}) collective-permute-start(bf16[768,256]{1,0:T(8,128)(2,1)S(1)} %reshape.12.own), channel_id=1, source_target_pairs={{0,1},{1,0},{2,3},{3,2},{4,5},{5,4},{6,7},{7,6},{8,9},{9,8},{10,11... | collective-permute-start | bytes 1179656 | tf_op jit(solution)/shard_map/ppermute | solution.py:167
  78.3 1.1 %collective-permute-done.3.far = bf16[768,256]{1,0:T(8,128)(2,1)S(1)} collective-permute-done((bf16[768,256]{1,0:T(8,128)(2,1)S(1)}, bf16[768,256]{1,0:T(8,128)(2,1)S(1)}, u32[]{:S(2)}, u32[]{:S(2)}) %collective-permute-start.3) | collective-permute-done | bytes 393248 | tf_op jit(solution)/shard_map/ppermute | solution.py:166
  79.5 5.6 %collective-permute-start.4 = (bf16[768,256]{1,0:T(8,128)(2,1)S(1)}, bf16[768,256]{1,0:T(8,128)(2,1)S(1)}, u32[]{:S(2)}, u32[]{:S(2)}) collective-permute-start(bf16[768,256]{1,0:T(8,128)(2,1)S(1)} %collective-permute-done.3.far), channel_id=1, source_target_pairs={{0,1},{1,0},{2,3},{3,2},{4,5},{5,4},{6,7},{7,6},{8,9},{9,8},{10,11... | collective-permute-start | bytes 1179656 | tf_op jit(solution)/shard_map/ppermute | solution.py:168
  85.1 0.0 collective-permute-done.2.side
  85.1 1.3 %collective-permute-done.4.far_side = bf16[768,256]{1,0:T(8,128)(2,1)S(1)} collective-permute-done((bf16[768,256]{1,0:T(8,128)(2,1)S(1)}, bf16[768,256]{1,0:T(8,128)(2,1)S(1)}, u32[]{:S(2)}, u32[]{:S(2)}) %collective-permute-start.4) | collective-permute-done | bytes 393248 | tf_op jit(solution)/shard_map/ppermute | solution.py:168
  86.4 1.8 %shard_map.29 = f32[1,256,1024]{2,1,0:T(8,128)} custom-call(s32[1]{0:T(128)} %bitcast.place, bf16[768,256]{1,0:T(8,128)(2,1)S(1)} %reshape.12.own, bf16[768,256]{1,0:T(8,128)(2,1)S(1)} %collective-permute-done.2.side, bf16[768,256]{1,0:T(8,128)(2,1)S(1)} %collective-permute-done.3.far, bf16[768,256]{1,0:T(8,128)(2,1)S(1)} %collective-permute-done.4.far_side), custom_call_target="tpu_custom_call" | custom-call | flops 503316480 | bytes 2621440 | tf_op jit(solution)/shard_map/pallas_call | solution.py:135
  (1 shorter events, 0.0 us)
Async XLA Ops:
  0.0 1.9 %copy-start = (bf16[3,2048,256]{2,1,0:T(8,128)(2,1)S(1)}, bf16[3,2048,256]{2,1,0:T(8,128)(2,1)}, u32[]{:S(2)}) copy-start(bf16[3,2048,256]{2,1,0:T(8,128)(2,1)} %volts.1) | copy-start | bytes 9437188
  7.5 30.4 %copy-start.1 = (f32[128,256]{1,0:T(8,128)S(1)}, f32[128,256]{1,0:T(8,128)}, u32[]{:S(2)}) copy-start(f32[128,256]{1,0:T(8,128)} %param.3) | copy-start | bytes 393220
  7.5 30.2 %collective-permute-start = (f32[2,256,256]{2,1,0:T(8,128)S(1)}, f32[2,256,256]{2,1,0:T(8,128)S(1)}, u32[]{:S(2)}, u32[]{:S(2)}) collective-permute-start(f32[2,256,256]{2,1,0:T(8,128)S(1)} %get-tuple-element.9), channel_id=1, source_target_pairs={{0,4},{4,8},{8,12},{12,16},{16,20},{20,24},{24,28},{28,32},{32,36}... | collective-permute-start | bytes 1572872 | tf_op jit(solution)/shard_map/ppermute | solution.py:156
  12.5 25.2 %collective-permute-start.1 = (f32[1,256,256]{2,1,0:T(8,128)S(1)}, f32[1,256,256]{2,1,0:T(8,128)S(1)}, u32[]{:S(2)}, u32[]{:S(2)}) collective-permute-start(f32[1,256,256]{2,1,0:T(8,128)S(1)} %get-tuple-element.10), channel_id=1, source_target_pairs={{0,508},{4,0},{8,4},{12,8},{16,12},{20,16},{24,20},{28,24},{32,28}... | collective-permute-start | bytes 786440 | tf_op jit(solution)/shard_map/ppermute | solution.py:157
  66.3 13.1 %collective-permute-start.3 = (bf16[768,256]{1,0:T(8,128)(2,1)S(1)}, bf16[768,256]{1,0:T(8,128)(2,1)S(1)}, u32[]{:S(2)}, u32[]{:S(2)}) collective-permute-start(bf16[768,256]{1,0:T(8,128)(2,1)S(1)} %reshape.12.own), channel_id=1, source_target_pairs={{0,2},{1,3},{2,0},{3,1},{4,6},{5,7},{6,4},{7,5},{8,10},{9,11},{10,... | collective-permute-start | bytes 1179656 | tf_op jit(solution)/shard_map/ppermute | solution.py:166
  73.1 12.0 %collective-permute-start.2 = (bf16[768,256]{1,0:T(8,128)(2,1)S(1)}, bf16[768,256]{1,0:T(8,128)(2,1)S(1)}, u32[]{:S(2)}, u32[]{:S(2)}) collective-permute-start(bf16[768,256]{1,0:T(8,128)(2,1)S(1)} %reshape.12.own), channel_id=1, source_target_pairs={{0,1},{1,0},{2,3},{3,2},{4,5},{5,4},{6,7},{7,6},{8,9},{9,8},{10,11... | collective-permute-start | bytes 1179656 | tf_op jit(solution)/shard_map/ppermute | solution.py:167
  79.5 6.9 %collective-permute-start.4 = (bf16[768,256]{1,0:T(8,128)(2,1)S(1)}, bf16[768,256]{1,0:T(8,128)(2,1)S(1)}, u32[]{:S(2)}, u32[]{:S(2)}) collective-permute-start(bf16[768,256]{1,0:T(8,128)(2,1)S(1)} %collective-permute-done.3.far), channel_id=1, source_target_pairs={{0,1},{1,0},{2,3},{3,2},{4,5},{5,4},{6,7},{7,6},{8,9},{9,8},{10,11... | collective-permute-start | bytes 1179656 | tf_op jit(solution)/shard_map/ppermute | solution.py:168

commit v2 on v1

v2 whole, which is shorter than its diff:
```python
import functools
import math

import jax
import jax.numpy as jnp
from jax import lax
from jax.experimental import pallas as pl
from jax.experimental.pallas import tpu as pltpu
from jax.sharding import PartitionSpec as P

TAPS = 4
LANES = 128


def tap_window(frame_len):
    length = TAPS * frame_len
    shape = (length // LANES, LANES)
    sample = (
        lax.broadcasted_iota(jnp.int32, shape, 0) * LANES
        + lax.broadcasted_iota(jnp.int32, shape, 1)
    ).astype(jnp.float32)
    angle = math.pi * ((sample - length / 2 + 0.5) / frame_len)
    window = jnp.sin(angle) / angle * (
        0.5 - 0.5 * jnp.cos(2.0 * math.pi * (sample + 0.5) / length)
    )
    return window / jnp.sqrt(jnp.sum(window * window))


def fill_table(window_ref, table_ref, frame_len, channels):
    window_ref[...] = tap_window(frame_len)
    first_channel = (frame_len // 2 - channels) // 2
    rows = frame_len // LANES
    shape = (channels, LANES)
    channel = first_channel + lax.broadcasted_iota(jnp.int32, shape, 0)
    lane = lax.broadcasted_iota(jnp.int32, shape, 1)
    low = (channel * lane % frame_len).astype(jnp.float32) * (2.0 * math.pi / frame_len)
    cos_low, sin_low = jnp.cos(low), jnp.sin(low)
    few = lax.broadcasted_iota(jnp.int32, (rows, LANES), 0) + first_channel
    part = lax.broadcasted_iota(jnp.int32, (rows, LANES), 1)
    high = (few * part % rows).astype(jnp.float32) * (2.0 * math.pi / rows)
    cos_high, sin_high = jnp.cos(high), jnp.sin(high)
    repeats = channels // rows

    def spread(values, h):
        column = jnp.broadcast_to(values[:, h : h + 1], (rows, LANES))
        return jnp.broadcast_to(column[None], (repeats, rows, LANES)).reshape(shape)

    for h in range(rows):
        cos_h, sin_h = spread(cos_high, h), spread(sin_high, h)
        cos_all = cos_low * cos_h - sin_low * sin_h
        sin_all = -(sin_low * cos_h + cos_low * sin_h)
        for k in range(TAPS):
            weight = window_ref[k * rows + h : k * rows + h + 1, :]
            at = slice(h * LANES, (h + 1) * LANES)
            table_ref[k, :channels, at] = (cos_all * weight).astype(jnp.bfloat16)
            table_ref[k, channels:, at] = (sin_all * weight).astype(jnp.bfloat16)


def partial_kernel(volts, chunks, frames, table, window, rows, sems):
    count, frame_len, width = frames.shape
    channels = table.shape[1] // 2
    halves = width // LANES
    touched = count + TAPS - 1
    copies = [pltpu.make_async_copy(volts.at[f], frames.at[f], sems.at[f]) for f in range(count)]
    for copy in copies:
        copy.start()
    fill_table(window, table, frame_len, channels)
    for copy in copies:
        copy.wait()
    for s in range(touched):
        total = None
        for f in range(count):
            k = f + TAPS - 1 - s
            if 0 <= k < TAPS:
                product = jnp.dot(table[k], frames[f], preferred_element_type=jnp.float32)
                total = product if total is None else total + product
        for p in range(2):
            for h in range(halves):
                at = ((s * 2 + p) * halves + h) * channels
                rows[at : at + channels, :] = total[
                    p * channels : (p + 1) * channels, h * LANES : (h + 1) * LANES
                ]
    size = touched * 2 * halves
    together = 2

    def turn(step, carry):
        pieces = [
            rows[pl.ds(j * channels + step * together + q, 8, stride=channels), :]
            for q in range(together)
            for j in range(0, size, 8)
        ]
        start = pl.multiple_of(step * (together * size), together * size)
        chunks[pl.ds(start, together * size), :] = jnp.concatenate(pieces, 0).astype(jnp.bfloat16)
        return carry

    lax.fori_loop(0, channels // together, turn, 0, unroll=8)


def partial_spectra(voltages, channels):
    count, frame_len, width = voltages.shape
    size = (count + TAPS - 1) * 2 * (width // LANES)
    return pl.pallas_call(
        partial_kernel,
        out_shape=jax.ShapeDtypeStruct((channels * size, LANES), jnp.bfloat16),
        in_specs=[pl.BlockSpec(memory_space=pl.ANY)],
        out_specs=pl.BlockSpec(memory_space=pltpu.VMEM),
        scratch_shapes=[
            pltpu.VMEM((count, frame_len, width), jnp.bfloat16),
            pltpu.VMEM((TAPS, 2 * channels, frame_len), jnp.bfloat16),
            pltpu.VMEM((TAPS * frame_len // LANES, LANES), jnp.float32),
            pltpu.VMEM((size * channels, LANES), jnp.float32),
            pltpu.SemaphoreType.DMA((count,)),
        ],
        compiler_params=pltpu.CompilerParams(vmem_limit_bytes=60 * 1024 * 1024),
        cost_estimate=pl.CostEstimate(
            flops=2 * 12 * 2 * channels * frame_len * width,
            bytes_accessed=voltages.size * 2 + channels * size * LANES * 2,
            transcendentals=0,
        ),
    )(voltages)


def finish_kernel(count, place, chunks, gain, spectra, wide):
    groups = spectra.shape[0] // (2 * count)
    halves = spectra.shape[1] // LANES
    size = chunks.shape[0] // groups
    begun = count * 2 * halves
    wide[:size, :] = jnp.zeros((size, LANES), jnp.float32)
    wide[size:, :] = chunks[...].astype(jnp.float32)
    scale = gain[pl.ds(place[0], 1), :]
    for sp in range(2 * count):
        for h in range(halves):
            r = sp * halves + h
            own = wide[pl.ds(size + r, groups, stride=size), :]
            before = wide[pl.ds(begun + r, groups, stride=size), :]
            lanes = slice(h * LANES, (h + 1) * LANES)
            spectra[sp * groups : (sp + 1) * groups, lanes] = (
                (own + before) * scale[:, lanes]
            ).astype(jnp.bfloat16)


def finished_spectra(place, chunks, channel_gain, count, groups):
    width = channel_gain.shape[1]
    return pl.pallas_call(
        functools.partial(finish_kernel, count),
        out_shape=jax.ShapeDtypeStruct((2 * count * groups, width), jnp.bfloat16),
        in_specs=[pl.BlockSpec(memory_space=pltpu.SMEM)]
        + [pl.BlockSpec(memory_space=pltpu.VMEM)] * 2,
        out_specs=pl.BlockSpec(memory_space=pltpu.VMEM),
        scratch_shapes=[
            pltpu.VMEM((chunks.shape[0] + chunks.shape[0] // groups, LANES), jnp.float32)
        ],
        compiler_params=pltpu.CompilerParams(vmem_limit_bytes=16 * 1024 * 1024),
    )(place, chunks, channel_gain)


def product(left, right):
    return jnp.dot(left, right, preferred_element_type=jnp.float32)


def near_kernel(groups, norm_scale, place, own, side, far, out, turned, block, sems):
    rows, width = own.shape
    mine = place[0]
    turned[0] = own[...].T
    for s in range(rows // (2 * groups)):
        real = slice(2 * s * groups, (2 * s + 1) * groups)
        imag = slice((2 * s + 1) * groups, (2 * s + 2) * groups)
        turned[1, :, real] = turned[0, :, imag]
        turned[1, :, imag] = -turned[0, :, real]
    copies = []

    def place_block(at, other, value):
        block[at] = value * norm_scale
        columns = pl.ds(pl.multiple_of(other * width, width), width)
        copies.append(pltpu.make_async_copy(block.at[at], out.at[0, :, columns], sems.at[at]))
        copies[-1].start()

    upper = lax.broadcasted_iota(jnp.int32, (width, width), 0) <= lax.broadcasted_iota(
        jnp.int32, (width, width), 1
    )
    place_block(
        0, mine, jnp.where(upper, product(turned[0], own[...]), product(turned[1], own[...]))
    )
    for at, flip, right in ((1, 1, side), (2, 2, far)):
        other = mine ^ flip
        part = (other < mine).astype(jnp.int32)
        place_block(at, other, product(turned[part], right[...]))
    for copy in copies:
        copy.wait()


def last_kernel(norm_scale, place, turned, far_side, begun, out, block, sem):
    width = far_side.shape[1]
    other = place[0] ^ 3
    part = (other < place[0]).astype(jnp.int32)
    block[...] = product(turned[part], far_side[...]) * norm_scale
    columns = pl.ds(pl.multiple_of(other * width, width), width)
    copy = pltpu.make_async_copy(block, out.at[0, :, columns], sem)
    copy.start()
    copy.wait()


def shards(voltages, channel_gain):
    count = voltages.shape[0]
    channels, width = channel_gain.shape
    groups = lax.axis_size("tf")
    norm_scale = 1.0 / math.sqrt(count * groups)
    group = lax.axis_index("tf").astype(jnp.int32).reshape(1)
    place = lax.axis_index("inp").astype(jnp.int32).reshape(1)
    chunks = partial_spectra(voltages, channels).reshape(channels, -1, LANES)
    turned = lax.all_to_all(chunks, "tf", split_axis=0, concat_axis=0, tiled=True)
    own = finished_spectra(group, turned.reshape(-1, LANES), channel_gain, count, groups)
    far = lax.ppermute(own, "inp", [(i, i ^ 2) for i in range(4)])
    side = lax.ppermute(own, "inp", [(i, i ^ 1) for i in range(4)])
    far_side = lax.ppermute(far, "inp", [(i, i ^ 1) for i in range(4)])
    in_smem = pl.BlockSpec(memory_space=pltpu.SMEM)
    in_vmem = pl.BlockSpec(memory_space=pltpu.VMEM)
    anywhere = pl.BlockSpec(memory_space=pl.ANY)
    shape = jax.ShapeDtypeStruct((1, width, 4 * width), jnp.float32)
    begun, left = pl.pallas_call(
        functools.partial(near_kernel, groups, norm_scale),
        out_shape=(shape, jax.ShapeDtypeStruct((2, width, own.shape[0]), jnp.bfloat16)),
        in_specs=[in_smem, in_vmem, in_vmem, in_vmem],
        out_specs=(anywhere, in_vmem),
        scratch_shapes=[
            pltpu.VMEM((3, width, width), jnp.float32),
            pltpu.SemaphoreType.DMA((3,)),
        ],
        compiler_params=pltpu.CompilerParams(vmem_limit_bytes=16 * 1024 * 1024),
        cost_estimate=pl.CostEstimate(
            flops=2 * 4 * own.size * width, bytes_accessed=6 * own.size, transcendentals=0
        ),
    )(place, own, side, far)
    return pl.pallas_call(
        functools.partial(last_kernel, norm_scale),
        out_shape=shape,
        in_specs=[in_smem, in_vmem, in_vmem, anywhere],
        out_specs=anywhere,
        scratch_shapes=[pltpu.VMEM((width, width), jnp.float32), pltpu.SemaphoreType.DMA],
        input_output_aliases={3: 0},
        compiler_params=pltpu.CompilerParams(vmem_limit_bytes=16 * 1024 * 1024),
        cost_estimate=pl.CostEstimate(
            flops=2 * own.size * width, bytes_accessed=2 * own.size, transcendentals=0
        ),
    )(place, left, far_side, begun)


def solution(mesh):
    placed = (P("tf", None, "inp"), P(None, "inp"))
    return jax.shard_map(
        shards, mesh=mesh, in_specs=placed, out_specs=P("tf", "inp", None), check_vma=False
    )
```

time: 88.5 us -> 73.1 us (0.83)
  blocking collectives: 27.8 us -> 0 us
  waiting for transfers between devices: 13.8 us -> 31.4 us
  starting transfers between devices: 36.4 us -> 31.4 us
  Pallas kernels: 7.44 us -> 9.96 us
  local copies, waits for them, and re-layouts: 2.45 us -> 0.01 us
    all_to_all x1 -> x0, blocking collectives: 27.8 us -> none  [shards(): lax.all_to_all(spectra, 'tf', split_axis=0, concat_axis=0, tiled=True)]
    all_to_all x0 -> x1, waiting for transfers between devices: none -> 26.7 us  [shards(): lax.all_to_all(chunks, 'tf', split_axis=0, concat_axis=0, tiled=True)]
    all_to_all x0 -> x1, starting transfers between devices: none -> 20.8 us  [shards(): lax.all_to_all(chunks, 'tf', split_axis=0, concat_axis=0, tiled=True)]
    ppermute x2 -> x0, starting transfers between devices: 18.8 us -> none  [the longest x1 13.8 us: shards(): lax.ppermute(back, 'tf', [(i, (i - 1) % groups) for i in range(groups)])]
    ppermute x2 -> x0, waiting for transfers between devices: 11.4 us -> none  [the longest x1 11.4 us: shards(): lax.ppermute(back, 'tf', [(i, (i - 1) % groups) for i in range(groups)])]
    ppermute x1, starting transfers between devices: 6.74 us -> 1.92 us  [shards(): far = lax.ppermute(own, 'inp', [(i, i ^ 2) for i in range(4)])]
    ppermute x1, waiting for transfers between devices: 1.12 us -> 4.76 us  [shards(): far = lax.ppermute(own, 'inp', [(i, i ^ 2) for i in range(4)])]
    pallas_call x2 -> x4, Pallas kernels: 7.44 us -> 9.96 us  [the longest x1 7.18 us: partial_spectra(): pl.pallas_call(partial_kernel, out_shape=jax.ShapeDtypeStruct((channels *...]
  transfers between devices with their start and end apart: 5 -> 4, of which waited for: 3 -> 2; matrix products, arithmetic and copies ran while one was open for 0% -> 0% of each run, Pallas kernels for 0% -> 2%
where the time goes in v2:
time: 73.1 us; the launch traced here: 72.8 us
  starting transfers between devices  31.4 us (43%)
  waiting for transfers between devices  31.4 us (43%)
  Pallas kernels  9.96 us (14%)
    all_to_all x1, waiting for transfers between devices, shards(): lax.all_to_all(chunks, 'tf', split_axis=0, concat_axis=0, tiled=True)  26.7 us
    all_to_all x1, starting transfers between devices, shards(): lax.all_to_all(chunks, 'tf', split_axis=0, concat_axis=0, tiled=True)  20.8 us
    pallas_call x1, Pallas kernels, partial_spectra(): pl.pallas_call(partial_kernel, out_shape=jax.ShapeDtypeStruct((channels *...  7.18 us
    ppermute x1, waiting for transfers between devices, shards(): far = lax.ppermute(own, 'inp', [(i, i ^ 2) for i in range(4)])  4.76 us
    ppermute x1, starting transfers between devices, shards(): far_side = lax.ppermute(far, 'inp', [(i, i ^ 1) for i in range(4)])  4.53 us
    ppermute x1, starting transfers between devices, shards(): side = lax.ppermute(own, 'inp', [(i, i ^ 1) for i in range(4)])  4.09 us
    ppermute x1, starting transfers between devices, shards(): far = lax.ppermute(own, 'inp', [(i, i ^ 2) for i in range(4)])  1.92 us
  transfers between devices with their start and end apart: 4, of which 2 were waited for; matrix products, arithmetic and copies ran while one was open for 0% of the time, Pallas kernels for 2%

profile of v2, /device:TPU:1, one launch (start us, length us, event | category | flops | bytes accessed | tf_op | source)
XLA Modules:
  0.0 72.8 jit_solution(8806547815526183617)
XLA Ops:
  0.0 0.0 copy-start
  0.0 7.2 %shard_map.28 = bf16[3072,128]{1,0:T(8,128)(2,1)} custom-call(bf16[3,2048,256]{2,1,0:T(8,128)(2,1)} %volts.1), custom_call_target="tpu_custom_call" | custom-call | flops 3221225472 | bytes 3932160 | tf_op jit(solution)/shard_map/pallas_call | solution.py:102
  7.2 20.8 %all-to-all-start = ((bf16[128,24,128]{2,1,0:T(8,128)(2,1)}), bf16[128,24,128]{2,1,0:T(8,128)(2,1)S(1)}, u32[]{:S(2)}, u32[]{:S(2)}) async-start(bf16[128,24,128]{2,1,0:T(8,128)(2,1)} %bitcast.5), calls=%async_computation | async-start | bytes 1572864 | tf_op jit(solution)/shard_map/all_to_all | solution.py:211
  28.0 26.7 %all-to-all-done = bf16[128,24,128]{2,1,0:T(8,128)(2,1)S(1)} async-done(((bf16[128,24,128]{2,1,0:T(8,128)(2,1)}), bf16[128,24,128]{2,1,0:T(8,128)(2,1)S(1)}, u32[]{:S(2)}, u32[]{:S(2)}) %all-to-all-start) | async-done | bytes 786464 | tf_op jit(solution)/shard_map/all_to_all | solution.py:211
  54.7 0.0 copy-done
  54.7 0.4 shard_map.29.own
  55.1 1.9 %collective-permute-start.1 = (bf16[768,256]{1,0:T(8,128)(2,1)S(1)}, bf16[768,256]{1,0:T(8,128)(2,1)S(1)}, u32[]{:S(2)}, u32[]{:S(2)}) collective-permute-start(bf16[768,256]{1,0:T(8,128)(2,1)S(1)} %shard_map.29.own), channel_id=1, source_target_pairs={{0,2},{1,3},{2,0},{3,1},{4,6},{5,7},{6,4},{7,5},{8,10},{9,11},{10,... | collective-permute-start | bytes 1179656 | tf_op jit(solution)/shard_map/ppermute | solution.py:213
  57.0 4.1 %collective-permute-start = (bf16[768,256]{1,0:T(8,128)(2,1)S(1)}, bf16[768,256]{1,0:T(8,128)(2,1)S(1)}, u32[]{:S(2)}, u32[]{:S(2)}) collective-permute-start(bf16[768,256]{1,0:T(8,128)(2,1)S(1)} %shard_map.29.own), channel_id=1, source_target_pairs={{0,1},{1,0},{2,3},{3,2},{4,5},{5,4},{6,7},{7,6},{8,9},{9,8},{10,11... | collective-permute-start | bytes 1179656 | tf_op jit(solution)/shard_map/ppermute | solution.py:214
  61.1 4.8 %collective-permute-done.1.far = bf16[768,256]{1,0:T(8,128)(2,1)S(1)} collective-permute-done((bf16[768,256]{1,0:T(8,128)(2,1)S(1)}, bf16[768,256]{1,0:T(8,128)(2,1)S(1)}, u32[]{:S(2)}, u32[]{:S(2)}) %collective-permute-start.1) | collective-permute-done | bytes 393248 | tf_op jit(solution)/shard_map/ppermute | solution.py:213
  65.9 4.5 %collective-permute-start.2 = (bf16[768,256]{1,0:T(8,128)(2,1)S(1)}, bf16[768,256]{1,0:T(8,128)(2,1)S(1)}, u32[]{:S(2)}, u32[]{:S(2)}) collective-permute-start(bf16[768,256]{1,0:T(8,128)(2,1)S(1)} %collective-permute-done.1.far), channel_id=1, source_target_pairs={{0,1},{1,0},{2,3},{3,2},{4,5},{5,4},{6,7},{7,6},{8,9},{9,8},{10,11... | collective-permute-start | bytes 1179656 | tf_op jit(solution)/shard_map/ppermute | solution.py:215
  70.4 0.0 collective-permute-done.side
  70.4 1.4 %shard_map.30 = (f32[1,256,1024]{2,1,0:T(8,128)}, bf16[2,256,768]{2,1,0:T(8,128)(2,1)S(1)}) custom-call(s32[1]{0:T(128)} %bitcast.place, bf16[768,256]{1,0:T(8,128)(2,1)S(1)} %shard_map.29.own, bf16[768,256]{1,0:T(8,128)(2,1)S(1)} %collective-permute-done.side, bf16[768,256]{1,0:T(8,128)(2,1)S(1)} %collective-permute-done.1.far), custom_call_target="tpu_custom_call" | custom-call | flops 402653184 | bytes 1179648 | tf_op jit(solution)/shard_map/pallas_call | solution.py:220
  71.8 0.0 collective-permute-done.2.far_side
  71.9 1.0 %shard_map.31 = f32[1,256,1024]{2,1,0:T(8,128)} custom-call(s32[1]{0:T(128)} %bitcast.place, bf16[2,256,768]{2,1,0:T(8,128)(2,1)S(1)} %get-tuple-element.7.turned, bf16[768,256]{1,0:T(8,128)(2,1)S(1)} %collective-permute-done.2.far_side, f32[1,256,1024]{2,1,0:T(8,128)} %get-tuple-element.8.begun), custom_call_target="tpu_custom_call", output_to_operand_aliasing={{}: (3, {})} | custom-call | flops 100663296 | bytes 393216 | tf_op jit(solution)/shard_map/pallas_call | solution.py:234
Async XLA Ops:
  0.0 54.7 %copy-start = (f32[128,256]{1,0:T(8,128)S(1)}, f32[128,256]{1,0:T(8,128)}, u32[]{:S(2)}) copy-start(f32[128,256]{1,0:T(8,128)} %gain.1) | copy-start | bytes 393220
  7.2 47.5 %all-to-all-start = ((bf16[128,24,128]{2,1,0:T(8,128)(2,1)}), bf16[128,24,128]{2,1,0:T(8,128)(2,1)S(1)}, u32[]{:S(2)}, u32[]{:S(2)}) async-start(bf16[128,24,128]{2,1,0:T(8,128)(2,1)} %bitcast.5), calls=%async_computation | async-start | bytes 1572864 | tf_op jit(solution)/shard_map/all_to_all | solution.py:211
  55.1 10.8 %collective-permute-start.1 = (bf16[768,256]{1,0:T(8,128)(2,1)S(1)}, bf16[768,256]{1,0:T(8,128)(2,1)S(1)}, u32[]{:S(2)}, u32[]{:S(2)}) collective-permute-start(bf16[768,256]{1,0:T(8,128)(2,1)S(1)} %shard_map.29.own), channel_id=1, source_target_pairs={{0,2},{1,3},{2,0},{3,1},{4,6},{5,7},{6,4},{7,5},{8,10},{9,11},{10,... | collective-permute-start | bytes 1179656 | tf_op jit(solution)/shard_map/ppermute | solution.py:213
  57.0 13.4 %collective-permute-start = (bf16[768,256]{1,0:T(8,128)(2,1)S(1)}, bf16[768,256]{1,0:T(8,128)(2,1)S(1)}, u32[]{:S(2)}, u32[]{:S(2)}) collective-permute-start(bf16[768,256]{1,0:T(8,128)(2,1)S(1)} %shard_map.29.own), channel_id=1, source_target_pairs={{0,1},{1,0},{2,3},{3,2},{4,5},{5,4},{6,7},{7,6},{8,9},{9,8},{10,11... | collective-permute-start | bytes 1179656 | tf_op jit(solution)/shard_map/ppermute | solution.py:214
  65.9 6.0 %collective-permute-start.2 = (bf16[768,256]{1,0:T(8,128)(2,1)S(1)}, bf16[768,256]{1,0:T(8,128)(2,1)S(1)}, u32[]{:S(2)}, u32[]{:S(2)}) collective-permute-start(bf16[768,256]{1,0:T(8,128)(2,1)S(1)} %collective-permute-done.1.far), channel_id=1, source_target_pairs={{0,1},{1,0},{2,3},{3,2},{4,5},{5,4},{6,7},{7,6},{8,9},{9,8},{10,11... | collective-permute-start | bytes 1179656 | tf_op jit(solution)/shard_map/ppermute | solution.py:215

commit v3 on v2

--- a/solution.py
+++ b/solution.py
@@ -10,6 +10,26 @@
 
 TAPS = 4
 LANES = 128
+
+
+def sine_ratio_and_cosine(angle):
+    square = angle * angle
+
+    def series(start):
+        total = None
+        for n in range(start + 10, start - 1, -2):
+            term = (-1.0) ** (n // 2) / math.factorial(n)
+            total = term if total is None else total * square + term
+        return total
+
+    return series(1), series(2) * square + 1.0
+
+
+def cosine_and_sine(turns):
+    half = (turns - 0.5) * math.pi
+    ratio, cosine = sine_ratio_and_cosine(half)
+    sine = ratio * half
+    return 2.0 * sine * sine - 1.0, -2.0 * sine * cosine
 
 
 def tap_window(frame_len):
@@ -19,11 +39,11 @@
         lax.broadcasted_iota(jnp.int32, shape, 0) * LANES
         + lax.broadcasted_iota(jnp.int32, shape, 1)
     ).astype(jnp.float32)
-    angle = math.pi * ((sample - length / 2 + 0.5) / frame_len)
-    window = jnp.sin(angle) / angle * (
-        0.5 - 0.5 * jnp.cos(2.0 * math.pi * (sample + 0.5) / length)
-    )
-    return window / jnp.sqrt(jnp.sum(window * window))
+    w = (sample + (0.5 - length / 2)) * (math.pi / 4 / frame_len)
+    ratio, cosine = sine_ratio_and_cosine(w)
+    sine = ratio * w
+    window = ratio * (1.0 - 2.0 * sine * sine) * (cosine * cosine * cosine)
+    return window * lax.rsqrt(jnp.sum(window * window))
 
 
 def fill_table(window_ref, table_ref, frame_len, channels):
@@ -31,14 +51,19 @@
     first_channel = (frame_len // 2 - channels) // 2
     rows = frame_len // LANES
     shape = (channels, LANES)
-    channel = first_channel + lax.broadcasted_iota(jnp.int32, shape, 0)
-    lane = lax.broadcasted_iota(jnp.int32, shape, 1)
-    low = (channel * lane % frame_len).astype(jnp.float32) * (2.0 * math.pi / frame_len)
-    cos_low, sin_low = jnp.cos(low), jnp.sin(low)
-    few = lax.broadcasted_iota(jnp.int32, (rows, LANES), 0) + first_channel
-    part = lax.broadcasted_iota(jnp.int32, (rows, LANES), 1)
-    high = (few * part % rows).astype(jnp.float32) * (2.0 * math.pi / rows)
-    cos_high, sin_high = jnp.cos(high), jnp.sin(high)
+
+    def angles(count, step, start, scale, period):
+        row = lax.broadcasted_iota(jnp.int32, (count, LANES), 0) * step + start
+        lane = lax.broadcasted_iota(jnp.int32, (count, LANES), 1)
+        return cosine_and_sine((row * lane * scale % period).astype(jnp.float32) * (1.0 / period))
+
+    cos_i, sin_i = angles(channels // 8, 8, first_channel, 1, frame_len)
+    cos_j, sin_j = angles(8, 1, 0, 1, frame_len)
+    cos_i, sin_i = cos_i[:, None, :], sin_i[:, None, :]
+    cos_j, sin_j = cos_j[None], sin_j[None]
+    cos_low = (cos_i * cos_j - sin_i * sin_j).reshape(shape)
+    minus_sin_low = -(sin_i * cos_j + cos_i * sin_j).reshape(shape)
+    cos_high, sin_high = angles(rows, 1, first_channel, 1, rows)
     repeats = channels // rows
 
     def spread(values, h):
@@ -47,53 +72,81 @@
 
     for h in range(rows):
         cos_h, sin_h = spread(cos_high, h), spread(sin_high, h)
-        cos_all = cos_low * cos_h - sin_low * sin_h
-        sin_all = -(sin_low * cos_h + cos_low * sin_h)
+        cos_all = cos_low * cos_h + minus_sin_low * sin_h
+        minus_sin_all = minus_sin_low * cos_h - cos_low * sin_h
         for k in range(TAPS):
             weight = window_ref[k * rows + h : k * rows + h + 1, :]
-            at = slice(h * LANES, (h + 1) * LANES)
-            table_ref[k, :channels, at] = (cos_all * weight).astype(jnp.bfloat16)
-            table_ref[k, channels:, at] = (sin_all * weight).astype(jnp.bfloat16)
-
-
-def partial_kernel(volts, chunks, frames, table, window, rows, sems):
-    count, frame_len, width = frames.shape
-    channels = table.shape[1] // 2
+            at = slice(k * frame_len + h * LANES, k * frame_len + (h + 1) * LANES)
+            table_ref[:channels, at] = (cos_all * weight).astype(jnp.bfloat16)
+            table_ref[channels:, at] = (minus_sin_all * weight).astype(jnp.bfloat16)
+
+
+def partial_kernel(volts, chunks, frames, table, window, rows, turned, sems, out_sems):
+    count, frame_len, width = volts.shape
+    channels = table.shape[0] // 2
     halves = width // LANES
     touched = count + TAPS - 1
-    copies = [pltpu.make_async_copy(volts.at[f], frames.at[f], sems.at[f]) for f in range(count)]
+    pitch = channels + 8
+    copies = [
+        pltpu.make_async_copy(
+            volts.at[f], frames.at[f * frame_len : (f + 1) * frame_len], sems.at[f]
+        )
+        for f in range(count)
+    ]
+
+    def meet(first, last, s):
+        tap = first + TAPS - 1 - s
+        return jnp.dot(
+            table[:, tap * frame_len : (tap + last - first) * frame_len],
+            frames[first * frame_len : last * frame_len],
+            preferred_element_type=jnp.float32,
+        )
+
+    def store(s, total, add):
+        for p in range(2):
+            for h in range(halves):
+                at = ((s * 2 + p) * halves + h) * pitch
+                value = total[p * channels : (p + 1) * channels, h * LANES : (h + 1) * LANES]
+                if add:
+                    value = value + rows[at : at + channels, :]
+                rows[at : at + channels, :] = value
+
     for copy in copies:
         copy.start()
     fill_table(window, table, frame_len, channels)
-    for copy in copies:
+    copies[0].wait()
+    for s in range(TAPS):
+        store(s, meet(0, 1, s), False)
+    for copy in copies[1:]:
         copy.wait()
-    for s in range(touched):
-        total = None
-        for f in range(count):
-            k = f + TAPS - 1 - s
-            if 0 <= k < TAPS:
-                product = jnp.dot(table[k], frames[f], preferred_element_type=jnp.float32)
-                total = product if total is None else total + product
-        for p in range(2):
-            for h in range(halves):
-                at = ((s * 2 + p) * halves + h) * channels
-                rows[at : at + channels, :] = total[
-                    p * channels : (p + 1) * channels, h * LANES : (h + 1) * LANES
-                ]
+    for s in range(1, touched):
+        store(s, meet(max(1, s + 1 - TAPS), min(count, s + 1), s), s < TAPS)
+
     size = touched * 2 * halves
     together = 2
+    blocks = 4
+    steps = channels // together // blocks
 
     def turn(step, carry):
         pieces = [
-            rows[pl.ds(j * channels + step * together + q, 8, stride=channels), :]
+            rows[pl.ds(j * pitch + step * together + q, 8, stride=pitch), :]
             for q in range(together)
             for j in range(0, size, 8)
         ]
         start = pl.multiple_of(step * (together * size), together * size)
-        chunks[pl.ds(start, together * size), :] = jnp.concatenate(pieces, 0).astype(jnp.bfloat16)
+        turned[pl.ds(start, together * size), :] = jnp.concatenate(pieces, 0).astype(jnp.bfloat16)
         return carry
 
-    lax.fori_loop(0, channels // together, turn, 0, unroll=8)
+    out_copies = []
+    for block in range(blocks):
+        lax.fori_loop(block * steps, (block + 1) * steps, turn, 0, unroll=16)
+        part = pl.ds(block * steps * together * size, steps * together * size)
+        out_copies.append(
+            pltpu.make_async_copy(turned.at[part], chunks.at[part], out_sems.at[block])
+        )
+        out_copies[-1].start()
+    for copy in out_copies:
+        copy.wait()
 
 
 def partial_spectra(voltages, channels):
@@ -103,13 +156,15 @@
         partial_kernel,
         out_shape=jax.ShapeDtypeStruct((channels * size, LANES), jnp.bfloat16),
         in_specs=[pl.BlockSpec(memory_space=pl.ANY)],
-        out_specs=pl.BlockSpec(memory_space=pltpu.VMEM),
+        out_specs=pl.BlockSpec(memory_space=pl.ANY),
         scratch_shapes=[
-            pltpu.VMEM((count, frame_len, width), jnp.bfloat16),
-            pltpu.VMEM((TAPS, 2 * channels, frame_len), jnp.bfloat16),
+            pltpu.VMEM((count * frame_len, width), jnp.bfloat16),
+            pltpu.VMEM((2 * channels, TAPS * frame_len), jnp.bfloat16),
             pltpu.VMEM((TAPS * frame_len // LANES, LANES), jnp.float32),
-            pltpu.VMEM((size * channels, LANES), jnp.float32),
+            pltpu.VMEM(((size + 1) * (channels + 8), LANES), jnp.float32),
+            pltpu.VMEM((channels * size, LANES), jnp.bfloat16),
             pltpu.SemaphoreType.DMA((count,)),
+            pltpu.SemaphoreType.DMA((4,)),
         ],
         compiler_params=pltpu.CompilerParams(vmem_limit_bytes=60 * 1024 * 1024),
         cost_estimate=pl.CostEstimate(
@@ -126,7 +181,7 @@
     size = chunks.shape[0] // groups
     begun = count * 2 * halves
     wide[:size, :] = jnp.zeros((size, LANES), jnp.float32)
-    wide[size:, :] = chunks[...].astype(jnp.float32)
+    wide[size : size + chunks.shape[0], :] = chunks[...].astype(jnp.float32)
     scale = gain[pl.ds(place[0], 1), :]
     for sp in range(2 * count):
         for h in range(halves):
@@ -148,7 +203,7 @@
         + [pl.BlockSpec(memory_space=pltpu.VMEM)] * 2,
         out_specs=pl.BlockSpec(memory_space=pltpu.VMEM),
         scratch_shapes=[
-            pltpu.VMEM((chunks.shape[0] + chunks.shape[0] // groups, LANES), jnp.float32)
+            pltpu.VMEM((chunks.shape[0] // groups * (groups + 2), LANES), jnp.float32)
         ],
         compiler_params=pltpu.CompilerParams(vmem_limit_bytes=16 * 1024 * 1024),
     )(place, chunks, channel_gain)

time: 73.1 us -> 71.9 us (0.984)
  Pallas kernels: 9.96 us -> 8.76 us
    pallas_call x1, Pallas kernels: 7.18 us -> 5.99 us  [partial_spectra(): pl.pallas_call(partial_kernel, out_shape=jax.ShapeDtypeStruct((channels *...]
where the time goes in v3:
time: 71.9 us; the launch traced here: 71.6 us
  starting transfers between devices  31.4 us (44%)
  waiting for transfers between devices  31.4 us (44%)
  Pallas kernels  8.76 us (12%)
    all_to_all x1, waiting for transfers between devices, shards(): lax.all_to_all(chunks, 'tf', split_axis=0, concat_axis=0, tiled=True)  26.6 us
    all_to_all x1, starting transfers between devices, shards(): lax.all_to_all(chunks, 'tf', split_axis=0, concat_axis=0, tiled=True)  20.8 us
    pallas_call x1, Pallas kernels, partial_spectra(): pl.pallas_call(partial_kernel, out_shape=jax.ShapeDtypeStruct((channels *...  5.99 us
    ppermute x1, waiting for transfers between devices, shards(): far = lax.ppermute(own, 'inp', [(i, i ^ 2) for i in range(4)])  4.73 us
    ppermute x1, starting transfers between devices, shards(): far_side = lax.ppermute(far, 'inp', [(i, i ^ 1) for i in range(4)])  4.54 us
    ppermute x1, starting transfers between devices, shards(): side = lax.ppermute(own, 'inp', [(i, i ^ 1) for i in range(4)])  4.12 us
    ppermute x1, starting transfers between devices, shards(): far = lax.ppermute(own, 'inp', [(i, i ^ 2) for i in range(4)])  1.92 us
  transfers between devices with their start and end apart: 4, of which 2 were waited for; matrix products, arithmetic and copies ran while one was open for 0% of the time, Pallas kernels for 2%

profile of v3, /device:TPU:1, one launch (start us, length us, event | category | flops | bytes accessed | tf_op | source)
XLA Modules:
  0.0 71.6 jit_solution(7859647198506988878)
XLA Ops:
  0.0 0.0 copy-start
  0.0 6.0 %shard_map.28 = bf16[3072,128]{1,0:T(8,128)(2,1)} custom-call(bf16[3,2048,256]{2,1,0:T(8,128)(2,1)} %volts.1), custom_call_target="tpu_custom_call" | custom-call | flops 3221225472 | bytes 3932160 | tf_op jit(solution)/shard_map/pallas_call | solution.py:155
  6.0 20.8 %all-to-all-start = ((bf16[128,24,128]{2,1,0:T(8,128)(2,1)}), bf16[128,24,128]{2,1,0:T(8,128)(2,1)S(1)}, u32[]{:S(2)}, u32[]{:S(2)}) async-start(bf16[128,24,128]{2,1,0:T(8,128)(2,1)} %bitcast.5), calls=%async_computation | async-start | bytes 1572864 | tf_op jit(solution)/shard_map/all_to_all | solution.py:266
  26.8 26.6 %all-to-all-done = bf16[128,24,128]{2,1,0:T(8,128)(2,1)S(1)} async-done(((bf16[128,24,128]{2,1,0:T(8,128)(2,1)}), bf16[128,24,128]{2,1,0:T(8,128)(2,1)S(1)}, u32[]{:S(2)}, u32[]{:S(2)}) %all-to-all-start) | async-done | bytes 786464 | tf_op jit(solution)/shard_map/all_to_all | solution.py:266
  53.5 0.0 copy-done
  53.5 0.4 shard_map.29.own
  53.8 1.9 %collective-permute-start.1 = (bf16[768,256]{1,0:T(8,128)(2,1)S(1)}, bf16[768,256]{1,0:T(8,128)(2,1)S(1)}, u32[]{:S(2)}, u32[]{:S(2)}) collective-permute-start(bf16[768,256]{1,0:T(8,128)(2,1)S(1)} %shard_map.29.own), channel_id=1, source_target_pairs={{0,2},{1,3},{2,0},{3,1},{4,6},{5,7},{6,4},{7,5},{8,10},{9,11},{10,... | collective-permute-start | bytes 1179656 | tf_op jit(solution)/shard_map/ppermute | solution.py:268
  55.8 4.1 %collective-permute-start = (bf16[768,256]{1,0:T(8,128)(2,1)S(1)}, bf16[768,256]{1,0:T(8,128)(2,1)S(1)}, u32[]{:S(2)}, u32[]{:S(2)}) collective-permute-start(bf16[768,256]{1,0:T(8,128)(2,1)S(1)} %shard_map.29.own), channel_id=1, source_target_pairs={{0,1},{1,0},{2,3},{3,2},{4,5},{5,4},{6,7},{7,6},{8,9},{9,8},{10,11... | collective-permute-start | bytes 1179656 | tf_op jit(solution)/shard_map/ppermute | solution.py:269
  59.9 4.7 %collective-permute-done.1.far = bf16[768,256]{1,0:T(8,128)(2,1)S(1)} collective-permute-done((bf16[768,256]{1,0:T(8,128)(2,1)S(1)}, bf16[768,256]{1,0:T(8,128)(2,1)S(1)}, u32[]{:S(2)}, u32[]{:S(2)}) %collective-permute-start.1) | collective-permute-done | bytes 393248 | tf_op jit(solution)/shard_map/ppermute | solution.py:268
  64.6 4.5 %collective-permute-start.2 = (bf16[768,256]{1,0:T(8,128)(2,1)S(1)}, bf16[768,256]{1,0:T(8,128)(2,1)S(1)}, u32[]{:S(2)}, u32[]{:S(2)}) collective-permute-start(bf16[768,256]{1,0:T(8,128)(2,1)S(1)} %collective-permute-done.1.far), channel_id=1, source_target_pairs={{0,1},{1,0},{2,3},{3,2},{4,5},{5,4},{6,7},{7,6},{8,9},{9,8},{10,11... | collective-permute-start | bytes 1179656 | tf_op jit(solution)/shard_map/ppermute | solution.py:270
  69.2 0.0 collective-permute-done.side
  69.2 1.4 %shard_map.30 = (f32[1,256,1024]{2,1,0:T(8,128)}, bf16[2,256,768]{2,1,0:T(8,128)(2,1)S(1)}) custom-call(s32[1]{0:T(128)} %bitcast.place, bf16[768,256]{1,0:T(8,128)(2,1)S(1)} %shard_map.29.own, bf16[768,256]{1,0:T(8,128)(2,1)S(1)} %collective-permute-done.side, bf16[768,256]{1,0:T(8,128)(2,1)S(1)} %collective-permute-done.1.far), custom_call_target="tpu_custom_call" | custom-call | flops 402653184 | bytes 1179648 | tf_op jit(solution)/shard_map/pallas_call | solution.py:275
  70.6 0.0 collective-permute-done.2.far_side
  70.6 1.0 %shard_map.31 = f32[1,256,1024]{2,1,0:T(8,128)} custom-call(s32[1]{0:T(128)} %bitcast.place, bf16[2,256,768]{2,1,0:T(8,128)(2,1)S(1)} %get-tuple-element.7.turned, bf16[768,256]{1,0:T(8,128)(2,1)S(1)} %collective-permute-done.2.far_side, f32[1,256,1024]{2,1,0:T(8,128)} %get-tuple-element.8.begun), custom_call_target="tpu_custom_call", output_to_operand_aliasing={{}: (3, {})} | custom-call | flops 100663296 | bytes 393216 | tf_op jit(solution)/shard_map/pallas_call | solution.py:289
Async XLA Ops:
  0.0 53.5 %copy-start = (f32[128,256]{1,0:T(8,128)S(1)}, f32[128,256]{1,0:T(8,128)}, u32[]{:S(2)}) copy-start(f32[128,256]{1,0:T(8,128)} %gain.1) | copy-start | bytes 393220
  6.0 47.5 %all-to-all-start = ((bf16[128,24,128]{2,1,0:T(8,128)(2,1)}), bf16[128,24,128]{2,1,0:T(8,128)(2,1)S(1)}, u32[]{:S(2)}, u32[]{:S(2)}) async-start(bf16[128,24,128]{2,1,0:T(8,128)(2,1)} %bitcast.5), calls=%async_computation | async-start | bytes 1572864 | tf_op jit(solution)/shard_map/all_to_all | solution.py:266
  53.8 10.8 %collective-permute-start.1 = (bf16[768,256]{1,0:T(8,128)(2,1)S(1)}, bf16[768,256]{1,0:T(8,128)(2,1)S(1)}, u32[]{:S(2)}, u32[]{:S(2)}) collective-permute-start(bf16[768,256]{1,0:T(8,128)(2,1)S(1)} %shard_map.29.own), channel_id=1, source_target_pairs={{0,2},{1,3},{2,0},{3,1},{4,6},{5,7},{6,4},{7,5},{8,10},{9,11},{10,... | collective-permute-start | bytes 1179656 | tf_op jit(solution)/shard_map/ppermute | solution.py:268
  55.8 13.4 %collective-permute-start = (bf16[768,256]{1,0:T(8,128)(2,1)S(1)}, bf16[768,256]{1,0:T(8,128)(2,1)S(1)}, u32[]{:S(2)}, u32[]{:S(2)}) collective-permute-start(bf16[768,256]{1,0:T(8,128)(2,1)S(1)} %shard_map.29.own), channel_id=1, source_target_pairs={{0,1},{1,0},{2,3},{3,2},{4,5},{5,4},{6,7},{7,6},{8,9},{9,8},{10,11... | collective-permute-start | bytes 1179656 | tf_op jit(solution)/shard_map/ppermute | solution.py:269
  64.6 6.0 %collective-permute-start.2 = (bf16[768,256]{1,0:T(8,128)(2,1)S(1)}, bf16[768,256]{1,0:T(8,128)(2,1)S(1)}, u32[]{:S(2)}, u32[]{:S(2)}) collective-permute-start(bf16[768,256]{1,0:T(8,128)(2,1)S(1)} %collective-permute-done.1.far), channel_id=1, source_target_pairs={{0,1},{1,0},{2,3},{3,2},{4,5},{5,4},{6,7},{7,6},{8,9},{9,8},{10,11... | collective-permute-start | bytes 1179656 | tf_op jit(solution)/shard_map/ppermute | solution.py:270

commit v4 on v3

--- a/solution.py
+++ b/solution.py
@@ -10,6 +10,8 @@
 
 TAPS = 4
 LANES = 128
+LONG = 4
+DEEP = 8
 
 
 def sine_ratio_and_cosine(angle):
@@ -128,8 +130,11 @@
     steps = channels // together // blocks
 
     def turn(step, carry):
+        first = step * together
+        place = first // LONG
+        channel = place // DEEP * (LONG * DEEP) + first % LONG * DEEP + place % DEEP
         pieces = [
-            rows[pl.ds(j * pitch + step * together + q, 8, stride=pitch), :]
+            rows[pl.ds(j * pitch + channel + q * DEEP, 8, stride=pitch), :]
             for q in range(together)
             for j in range(0, size, 8)
         ]
@@ -175,84 +180,159 @@
     )(voltages)
 
 
-def finish_kernel(count, place, chunks, gain, spectra, wide):
-    groups = spectra.shape[0] // (2 * count)
-    halves = spectra.shape[1] // LANES
-    size = chunks.shape[0] // groups
-    begun = count * 2 * halves
-    wide[:size, :] = jnp.zeros((size, LANES), jnp.float32)
-    wide[size : size + chunks.shape[0], :] = chunks[...].astype(jnp.float32)
-    scale = gain[pl.ds(place[0], 1), :]
-    for sp in range(2 * count):
-        for h in range(halves):
-            r = sp * halves + h
-            own = wide[pl.ds(size + r, groups, stride=size), :]
-            before = wide[pl.ds(begun + r, groups, stride=size), :]
-            lanes = slice(h * LANES, (h + 1) * LANES)
-            spectra[sp * groups : (sp + 1) * groups, lanes] = (
-                (own + before) * scale[:, lanes]
-            ).astype(jnp.bfloat16)
-
-
-def finished_spectra(place, chunks, channel_gain, count, groups):
-    width = channel_gain.shape[1]
+def gather_kernel(count, place, chunks, gain, pieces, wide, ends):
+    halves = gain.shape[1] // LANES
+    half = count * 2 * halves
+    size = 2 * half
+    block = LONG * size
+    sources = chunks.shape[0] // block
+    runs = sources // DEEP
+    length = half * (sources + runs)
+    pitch = block + 8
+    wide[:pitch, :] = jnp.zeros((pitch, LANES), jnp.float32)
+    for source in range(sources):
+        at = (source + 1) * pitch
+        wide[at : at + block, :] = chunks[source * block : (source + 1) * block, :].astype(jnp.float32)
+    inner = lax.broadcasted_iota(jnp.int32, (sources, LANES), 0) % DEEP > 0
+    odd = lax.broadcasted_iota(jnp.int32, (half, LANES), 0) % halves
+    for x in range(LONG):
+        scale = gain[pl.ds(place[0] + x * DEEP, 1), :]
+        first = x * 2 * length
+        for r in range(half):
+            h = r % halves
+            own = wide[pl.ds(pitch + x * size + r, sources, stride=pitch), :]
+            before = wide[pl.ds(x * size + half + r, sources, stride=pitch), :]
+            value = (own + jnp.where(inner, before, 0.0)) * scale[:, h * LANES : (h + 1) * LANES]
+            for copy in range(2):
+                at = first + copy * length + r * sources
+                pieces[at : at + sources, :] = value.astype(jnp.bfloat16)
+        scales = scale[:, :LANES]
+        for h in range(1, halves):
+            scales = jnp.where(odd == h, scale[:, h * LANES : (h + 1) * LANES], scales)
+        for y in range(runs):
+            at = (y * DEEP + DEEP) * pitch + x * size + half
+            ends[y * half : (y + 1) * half, :] = wide[at : at + half, :] * scales
+        for copy in range(2):
+            at = first + copy * length + half * sources
+            pieces[at : at + half * runs, :] = ends[...].astype(jnp.bfloat16)
+
+
+def gathered_pieces(place, chunks, channel_gain, count):
+    half = count * 2 * (channel_gain.shape[1] // LANES)
+    block = LONG * 2 * half
+    sources = chunks.shape[0] // block
+    runs = sources // DEEP
     return pl.pallas_call(
-        functools.partial(finish_kernel, count),
-        out_shape=jax.ShapeDtypeStruct((2 * count * groups, width), jnp.bfloat16),
+        functools.partial(gather_kernel, count),
+        out_shape=jax.ShapeDtypeStruct((2 * LONG * half * (sources + runs), LANES), jnp.bfloat16),
         in_specs=[pl.BlockSpec(memory_space=pltpu.SMEM)]
         + [pl.BlockSpec(memory_space=pltpu.VMEM)] * 2,
         out_specs=pl.BlockSpec(memory_space=pltpu.VMEM),
         scratch_shapes=[
-            pltpu.VMEM((chunks.shape[0] // groups * (groups + 2), LANES), jnp.float32)
+            pltpu.VMEM(((block + 8) * (sources + 3), LANES), jnp.float32),
+            pltpu.VMEM((half * runs, LANES), jnp.float32),
         ],
         compiler_params=pltpu.CompilerParams(vmem_limit_bytes=16 * 1024 * 1024),
     )(place, chunks, channel_gain)
 
 
+def column_kernel(count, sources, pieces, column, carried):
+    width = column.shape[1]
+    halves = width // LANES
+    half = count * 2 * halves
+    runs = sources // DEEP
+    length = half * (sources + runs)
+    steps = LONG * sources
+    first_of_run = lax.broadcasted_iota(jnp.int32, (LONG * runs, DEEP, LANES), 1) == 0
+    for chip in range(2):
+        carried[:half, :] = jnp.zeros((half, LANES), jnp.float32)
+        for x in range(LONG):
+            for y in range(runs):
+                run = y * LONG + x + 1
+                if run < LONG * runs:
+                    at = (x * 2 + chip) * length + half * sources + y * half
+                    to = (run % LONG * runs + run // LONG) * half
+                    carried[to : to + half, :] = pieces[at : at + half, :].astype(jnp.float32)
+        for r in range(half):
+            sp, h = r // halves, r % halves
+            own = jnp.concatenate(
+                [
+                    pieces[
+                        (x * 2 + chip) * length + r * sources : (x * 2 + chip) * length
+                        + (r + 1) * sources,
+                        :,
+                    ]
+                    for x in range(LONG)
+                ],
+                0,
+            ).astype(jnp.float32)
+            begun = carried[pl.ds(r, LONG * runs, stride=half), :]
+            begun = jnp.where(first_of_run, begun[:, None, :], 0.0).reshape(steps, LANES)
+            at = (chip * count * 2 + sp) * steps
+            column[at : at + steps, h * LANES : (h + 1) * LANES] = (own + begun).astype(
+                jnp.bfloat16
+            )
+
+
+def both_columns(pieces, count, width, groups):
+    half = count * 2 * (width // LANES)
+    sources = groups // LONG
+    return pl.pallas_call(
+        functools.partial(column_kernel, count, sources),
+        out_shape=jax.ShapeDtypeStruct((4 * count * groups, width), jnp.bfloat16),
+        in_specs=[pl.BlockSpec(memory_space=pltpu.VMEM)],
+        out_specs=pl.BlockSpec(memory_space=pltpu.VMEM),
+        scratch_shapes=[pltpu.VMEM((half * (groups // DEEP + 1), LANES), jnp.float32)],
+        compiler_params=pltpu.CompilerParams(vmem_limit_bytes=16 * 1024 * 1024),
+    )(pieces)
+
+
 def product(left, right):
     return jnp.dot(left, right, preferred_element_type=jnp.float32)
 
 
-def near_kernel(groups, norm_scale, place, own, side, far, out, turned, block, sems):
-    rows, width = own.shape
+def place_blocks(width, parts, out, block, sems):
+    copies = []
+    for at, (other, value) in enumerate(parts):
+        block[at] = value
+        columns = pl.ds(pl.multiple_of(other * width, width), width)
+        copies.append(pltpu.make_async_copy(block.at[at], out.at[0, :, columns], sems.at[at]))
+        copies[-1].start()
+    for copy in copies:
+        copy.wait()
+
+
+def near_kernel(groups, norm_scale, place, column, out, turned, block, sems):
+    rows, width = column.shape[0] // 2, column.shape[1]
     mine = place[0]
-    turned[0] = own[...].T
+    chip = mine // 2
+    own = column[pl.ds(pl.multiple_of(chip * rows, rows), rows), :]
+    far = column[pl.ds(pl.multiple_of((1 - chip) * rows, rows), rows), :]
+    turned[0] = own.T
     for s in range(rows // (2 * groups)):
         real = slice(2 * s * groups, (2 * s + 1) * groups)
         imag = slice((2 * s + 1) * groups, (2 * s + 2) * groups)
         turned[1, :, real] = turned[0, :, imag]
         turned[1, :, imag] = -turned[0, :, real]
-    copies = []
-
-    def place_block(at, other, value):
-        block[at] = value * norm_scale
-        columns = pl.ds(pl.multiple_of(other * width, width), width)
-        copies.append(pltpu.make_async_copy(block.at[at], out.at[0, :, columns], sems.at[at]))
-        copies[-1].start()
-
     upper = lax.broadcasted_iota(jnp.int32, (width, width), 0) <= lax.broadcasted_iota(
         jnp.int32, (width, width), 1
     )
-    place_block(
-        0, mine, jnp.where(upper, product(turned[0], own[...]), product(turned[1], own[...]))
-    )
-    for at, flip, right in ((1, 1, side), (2, 2, far)):
-        other = mine ^ flip
-        part = (other < mine).astype(jnp.int32)
-        place_block(at, other, product(turned[part], right[...]))
-    for copy in copies:
-        copy.wait()
-
-
-def last_kernel(norm_scale, place, turned, far_side, begun, out, block, sem):
-    width = far_side.shape[1]
-    other = place[0] ^ 3
-    part = (other < place[0]).astype(jnp.int32)
-    block[...] = product(turned[part], far_side[...]) * norm_scale
-    columns = pl.ds(pl.multiple_of(other * width, width), width)
-    copy = pltpu.make_async_copy(block, out.at[0, :, columns], sem)
-    copy.start()
-    copy.wait()
+    diagonal = jnp.where(upper, product(turned[0], own), product(turned[1], own))
+    other = mine ^ 2
+    beside = product(turned[(other < mine).astype(jnp.int32)], far)
+    parts = [(mine, diagonal * norm_scale), (other, beside * norm_scale)]
+    place_blocks(width, parts, out, block, sems)
+
+
+def last_kernel(norm_scale, place, turned, column, begun, out, block, sems):
+    rows, width = column.shape[0] // 2, column.shape[1]
+    mine = place[0]
+    parts = []
+    for chip in range(2):
+        other = (mine ^ 1) % 2 + 2 * chip
+        left = turned[(other < mine).astype(jnp.int32)]
+        parts.append((other, product(left, column[chip * rows : (chip + 1) * rows]) * norm_scale))
+    place_blocks(width, parts, out, block, sems)
 
 
 def shards(voltages, channel_gain):
@@ -260,44 +340,64 @@
     channels, width = channel_gain.shape
     groups = lax.axis_size("tf")
     norm_scale = 1.0 / math.sqrt(count * groups)
-    group = lax.axis_index("tf").astype(jnp.int32).reshape(1)
+    group = lax.axis_index("tf").astype(jnp.int32)
+    plane = LONG * DEEP
+    base = (group // plane * plane + group % DEEP).reshape(1)
     place = lax.axis_index("inp").astype(jnp.int32).reshape(1)
-    chunks = partial_spectra(voltages, channels).reshape(channels, -1, LANES)
-    turned = lax.all_to_all(chunks, "tf", split_axis=0, concat_axis=0, tiled=True)
-    own = finished_spectra(group, turned.reshape(-1, LANES), channel_gain, count, groups)
-    far = lax.ppermute(own, "inp", [(i, i ^ 2) for i in range(4)])
-    side = lax.ppermute(own, "inp", [(i, i ^ 1) for i in range(4)])
-    far_side = lax.ppermute(far, "inp", [(i, i ^ 1) for i in range(4)])
+    chunks = partial_spectra(voltages, channels).reshape(groups // LONG, -1, LANES)
+    wheres = range(groups // plane)
+    same_x = [
+        [y * plane + x * DEEP + z for y in wheres for z in range(DEEP)] for x in range(LONG)
+    ]
+    turned = lax.all_to_all(
+        chunks, "tf", split_axis=0, concat_axis=0, tiled=True, axis_index_groups=same_x
+    )
+    pieces = gathered_pieces(base, turned.reshape(-1, LANES), channel_gain, count)
+    same_yz = [
+        [(y * plane + x * DEEP + z) * 4 + chip * 2 + core for x in range(LONG) for chip in range(2)]
+        for y in wheres
+        for z in range(DEEP)
+        for core in range(2)
+    ]
+    spread = lax.all_to_all(
+        pieces.reshape(2 * LONG, -1, LANES),
+        ("tf", "inp"),
+        split_axis=0,
+        concat_axis=0,
+        tiled=True,
+        axis_index_groups=same_yz,
+    )
+    column = both_columns(spread.reshape(-1, LANES), count, width, groups)
+    other_column = lax.ppermute(column, "inp", [(i, i ^ 1) for i in range(4)])
+    rows = column.shape[0] // 2
     in_smem = pl.BlockSpec(memory_space=pltpu.SMEM)
     in_vmem = pl.BlockSpec(memory_space=pltpu.VMEM)
     anywhere = pl.BlockSpec(memory_space=pl.ANY)
     shape = jax.ShapeDtypeStruct((1, width, 4 * width), jnp.float32)
+    scratch = [pltpu.VMEM((2, width, width), jnp.float32), pltpu.SemaphoreType.DMA((2,))]
+    limits = pltpu.CompilerParams(vmem_limit_bytes=16 * 1024 * 1024)
+    cost = pl.CostEstimate(
+        flops=6 * rows * width * width, bytes_accessed=8 * rows * width, transcendentals=0
+    )
     begun, left = pl.pallas_call(
         functools.partial(near_kernel, groups, norm_scale),
-        out_shape=(shape, jax.ShapeDtypeStruct((2, width, own.shape[0]), jnp.bfloat16)),
-        in_specs=[in_smem, in_vmem, in_vmem, in_vmem],
+        out_shape=(shape, jax.ShapeDtypeStruct((2, width, rows), jnp.bfloat16)),
+        in_specs=[in_smem, in_vmem],
         out_specs=(anywhere, in_vmem),
-        scratch_shapes=[
-            pltpu.VMEM((3, width, width), jnp.float32),
-            pltpu.SemaphoreType.DMA((3,)),
-        ],
-        compiler_params=pltpu.CompilerParams(vmem_limit_bytes=16 * 1024 * 1024),
-        cost_estimate=pl.CostEstimate(
-            flops=2 * 4 * own.size * width, bytes_accessed=6 * own.size, transcendentals=0
-        ),
-    )(place, own, side, far)
+        scratch_shapes=scratch,
+        compiler_params=limits,
+        cost_estimate=cost,
+    )(place, column)
     return pl.pallas_call(
         functools.partial(last_kernel, norm_scale),
         out_shape=shape,
         in_specs=[in_smem, in_vmem, in_vmem, anywhere],
         out_specs=anywhere,
-        scratch_shapes=[pltpu.VMEM((width, width), jnp.float32), pltpu.SemaphoreType.DMA],
+        scratch_shapes=scratch,
         input_output_aliases={3: 0},
-        compiler_params=pltpu.CompilerParams(vmem_limit_bytes=16 * 1024 * 1024),
-        cost_estimate=pl.CostEstimate(
-            flops=2 * own.size * width, bytes_accessed=2 * own.size, transcendentals=0
-        ),
-    )(place, left, far_side, begun)
+        compiler_params=limits,
+        cost_estimate=cost,
+    )(place, left, other_column, begun)
 
 
 def solution(mesh):

time: 71.9 us -> 71.2 us (level)
  blocking collectives: 0 us -> 14.9 us
  starting transfers between devices: 31.4 us -> 22.3 us
  waiting for transfers between devices: 31.4 us -> 24.3 us
    all_to_all x0 -> x1, blocking collectives: none -> 14.9 us  [shards(): lax.all_to_all(pieces.reshape(2 * LONG, -1, LANES), ('tf', 'inp'), split_...]
    ppermute x3 -> x1, starting transfers between devices: 10.6 us -> 5.78 us  [shards(): other_column = lax.ppermute(column, 'inp', [(i, i ^ 1) for i in range(4)])]
    all_to_all x1, starting transfers between devices: 20.8 us -> 16.5 us  [shards(): lax.all_to_all(chunks, 'tf', split_axis=0, concat_axis=0, tiled=True, axi...]
    ppermute x3 -> x1, waiting for transfers between devices: 4.73 us -> 0.55 us  [shards(): other_column = lax.ppermute(column, 'inp', [(i, i ^ 1) for i in range(4)])]
    all_to_all x1, waiting for transfers between devices: 26.6 us -> 23.8 us  [shards(): lax.all_to_all(chunks, 'tf', split_axis=0, concat_axis=0, tiled=True, axi...]
  transfers between devices with their start and end apart: 4 -> 2, of which waited for: 2 -> 2; matrix products, arithmetic and copies ran while one was open for 0% -> 0% of each run, Pallas kernels for 2% -> 2%
where the time goes in v4:
time: 71.2 us; the launch traced here: 70.9 us
  waiting for transfers between devices  24.3 us (34%)
  starting transfers between devices  22.3 us (31%)
  blocking collectives  14.9 us (21%)
  Pallas kernels  9.24 us (13%)
    all_to_all x1, waiting for transfers between devices, shards(): lax.all_to_all(chunks, 'tf', split_axis=0, concat_axis=0, tiled=True, axi...  23.8 us
    all_to_all x1, starting transfers between devices, shards(): lax.all_to_all(chunks, 'tf', split_axis=0, concat_axis=0, tiled=True, axi...  16.5 us
    all_to_all x1, blocking collectives, shards(): lax.all_to_all(pieces.reshape(2 * LONG, -1, LANES), ('tf', 'inp'), split_...  14.9 us
    pallas_call x1, Pallas kernels, partial_spectra(): pl.pallas_call(partial_kernel, out_shape=jax.ShapeDtypeStruct((channels *...  5.99 us
    ppermute x1, starting transfers between devices, shards(): other_column = lax.ppermute(column, 'inp', [(i, i ^ 1) for i in range(4)])  5.78 us
  transfers between devices with their start and end apart: 2, of which 2 were waited for; matrix products, arithmetic and copies ran while one was open for 0% of the time, Pallas kernels for 2%

profile of v4, /device:TPU:1, one launch (start us, length us, event | category | flops | bytes accessed | tf_op | source)
XLA Modules:
  0.0 70.9 jit_solution(5668631208569924699)
XLA Ops:
  0.0 0.0 copy-start
  0.0 6.0 %shard_map.28 = bf16[3072,128]{1,0:T(8,128)(2,1)} custom-call(bf16[3,2048,256]{2,1,0:T(8,128)(2,1)} %volts.1), custom_call_target="tpu_custom_call" | custom-call | flops 3221225472 | bytes 3932160 | tf_op jit(solution)/shard_map/pallas_call | solution.py:160
  6.0 16.5 %all-to-all-start = ((bf16[32,96,128]{2,1,0:T(8,128)(2,1)}), bf16[32,96,128]{2,1,0:T(8,128)(2,1)S(1)}, u32[]{:S(2)}, u32[]{:S(2)}) async-start(bf16[32,96,128]{2,1,0:T(8,128)(2,1)} %bitcast.9), calls=%async_computation | async-start | bytes 1572864 | tf_op jit(solution)/shard_map/all_to_all | solution.py:352
  22.6 23.8 %all-to-all-done = bf16[32,96,128]{2,1,0:T(8,128)(2,1)S(1)} async-done(((bf16[32,96,128]{2,1,0:T(8,128)(2,1)}), bf16[32,96,128]{2,1,0:T(8,128)(2,1)S(1)}, u32[]{:S(2)}, u32[]{:S(2)}) %all-to-all-start) | async-done | bytes 786464 | tf_op jit(solution)/shard_map/all_to_all | solution.py:352
  46.4 0.0 copy-done
  46.4 0.4 shard_map.29
  46.7 14.9 %all_to_all.10 = bf16[8,432,128]{2,1,0:T(8,128)(2,1)S(1)} all-to-all(bf16[8,432,128]{2,1,0:T(8,128)(2,1)S(1)} %bitcast.7), channel_id=1, replica_groups={{0,2,32,34,64,66,96,98},{1,3,33,35,65,67,97,99},{4,6,36,38,68,70,100,10..., dimensions={0} | all-to-all | bytes 1769472 | tf_op jit(solution)/shard_map/all_to_all | solution.py:362
  61.7 0.4 shard_map.30.column
  62.1 5.8 %collective-permute-start = (bf16[1536,256]{1,0:T(8,128)(2,1)S(1)}, bf16[1536,256]{1,0:T(8,128)(2,1)S(1)}, u32[]{:S(2)}, u32[]{:S(2)}) collective-permute-start(bf16[1536,256]{1,0:T(8,128)(2,1)S(1)} %shard_map.30.column), channel_id=1, source_target_pairs={{0,1},{1,0},{2,3},{3,2},{4,5},{5,4},{6,7},{7,6},{8,9},{9,8},{10,11... | collective-permute-start | bytes 2359304 | tf_op jit(solution)/shard_map/ppermute | solution.py:371
  67.8 1.3 %shard_map.31 = (f32[1,256,1024]{2,1,0:T(8,128)}, bf16[2,256,768]{2,1,0:T(8,128)(2,1)S(1)}) custom-call(s32[1]{0:T(128)} %bitcast.place, bf16[1536,256]{1,0:T(8,128)(2,1)S(1)} %shard_map.30.column), custom_call_target="tpu_custom_call" | custom-call | flops 301989888 | bytes 1572864 | tf_op jit(solution)/shard_map/pallas_call | solution.py:382
  69.2 0.6 collective-permute-done.column
  69.7 1.2 %shard_map.32 = f32[1,256,1024]{2,1,0:T(8,128)} custom-call(s32[1]{0:T(128)} %bitcast.place, bf16[2,256,768]{2,1,0:T(8,128)(2,1)S(1)} %get-tuple-element.7.turned, bf16[1536,256]{1,0:T(8,128)(2,1)S(1)} %collective-permute-done.column, f32[1,256,1024]{2,1,0:T(8,128)} %get-tuple-element.8.begun), custom_call_target="tpu_custom_call", output_to_operand_aliasing={{}: (3, {})} | custom-call | flops 301989888 | bytes 1572864 | tf_op jit(solution)/shard_map/pallas_call | solution.py:391
Async XLA Ops:
  0.0 46.4 %copy-start = (f32[128,256]{1,0:T(8,128)S(1)}, f32[128,256]{1,0:T(8,128)}, u32[]{:S(2)}) copy-start(f32[128,256]{1,0:T(8,128)} %gain.1) | copy-start | bytes 393220
  6.0 40.4 %all-to-all-start = ((bf16[32,96,128]{2,1,0:T(8,128)(2,1)}), bf16[32,96,128]{2,1,0:T(8,128)(2,1)S(1)}, u32[]{:S(2)}, u32[]{:S(2)}) async-start(bf16[32,96,128]{2,1,0:T(8,128)(2,1)} %bitcast.9), calls=%async_computation | async-start | bytes 1572864 | tf_op jit(solution)/shard_map/all_to_all | solution.py:352
  62.1 7.7 %collective-permute-start = (bf16[1536,256]{1,0:T(8,128)(2,1)S(1)}, bf16[1536,256]{1,0:T(8,128)(2,1)S(1)}, u32[]{:S(2)}, u32[]{:S(2)}) collective-permute-start(bf16[1536,256]{1,0:T(8,128)(2,1)S(1)} %shard_map.30.column), channel_id=1, source_target_pairs={{0,1},{1,0},{2,3},{3,2},{4,5},{5,4},{6,7},{7,6},{8,9},{9,8},{10,11... | collective-permute-start | bytes 2359304 | tf_op jit(solution)/shard_map/ppermute | solution.py:371

commit v5 on v4

--- a/solution.py
+++ b/solution.py
@@ -48,7 +48,7 @@
     return window * lax.rsqrt(jnp.sum(window * window))
 
 
-def fill_table(window_ref, table_ref, frame_len, channels):
+def fill_table(window_ref, table_ref, frame_len, channels, halfway):
     window_ref[...] = tap_window(frame_len)
     first_channel = (frame_len // 2 - channels) // 2
     rows = frame_len // LANES
@@ -73,6 +73,8 @@
         return jnp.broadcast_to(column[None], (repeats, rows, LANES)).reshape(shape)
 
     for h in range(rows):
+        if h == rows // 2:
+            halfway()
         cos_h, sin_h = spread(cos_high, h), spread(sin_high, h)
         cos_all = cos_low * cos_h + minus_sin_low * sin_h
         minus_sin_all = minus_sin_low * cos_h - cos_low * sin_h
@@ -113,10 +115,14 @@
                     value = value + rows[at : at + channels, :]
                 rows[at : at + channels, :] = value
 
-    for copy in copies:
-        copy.start()
-    fill_table(window, table, frame_len, channels)
-    copies[0].wait()
+    copies[0].start()
+    copies[1].start()
+
+    def halfway():
+        copies[0].wait()
+        copies[2].start()
+
+    fill_table(window, table, frame_len, channels, halfway)
     for s in range(TAPS):
         store(s, meet(0, 1, s), False)
     for copy in copies[1:]:
@@ -247,12 +253,13 @@
     for chip in range(2):
         carried[:half, :] = jnp.zeros((half, LANES), jnp.float32)
         for x in range(LONG):
+            at = (x * 2 + chip) * length + half * sources
+            ends = pieces[at : at + half * runs, :].astype(jnp.float32)
             for y in range(runs):
                 run = y * LONG + x + 1
                 if run < LONG * runs:
-                    at = (x * 2 + chip) * length + half * sources + y * half
                     to = (run % LONG * runs + run // LONG) * half
-                    carried[to : to + half, :] = pieces[at : at + half, :].astype(jnp.float32)
+                    carried[to : to + half, :] = ends[y * half : (y + 1) * half]
         for r in range(half):
             sp, h = r // halves, r % halves
             own = jnp.concatenate(

time: 71.2 us -> 71.2 us (level)
  no operation moved by 1% of the time
where the time goes in v5:
time: 71.2 us; the launch traced here: 70.9 us
  waiting for transfers between devices  24.3 us (34%)
  starting transfers between devices  22.3 us (31%)
  blocking collectives  15 us (21%)
  Pallas kernels  9.14 us (13%)
    all_to_all x1, waiting for transfers between devices, shards(): lax.all_to_all(chunks, 'tf', split_axis=0, concat_axis=0, tiled=True, axi...  23.8 us
    all_to_all x1, starting transfers between devices, shards(): lax.all_to_all(chunks, 'tf', split_axis=0, concat_axis=0, tiled=True, axi...  16.5 us
    all_to_all x1, blocking collectives, shards(): lax.all_to_all(pieces.reshape(2 * LONG, -1, LANES), ('tf', 'inp'), split_...  15 us
    pallas_call x1, Pallas kernels, partial_spectra(): pl.pallas_call(partial_kernel, out_shape=jax.ShapeDtypeStruct((channels *...  5.89 us
    ppermute x1, starting transfers between devices, shards(): other_column = lax.ppermute(column, 'inp', [(i, i ^ 1) for i in range(4)])  5.77 us
  transfers between devices with their start and end apart: 2, of which 2 were waited for; matrix products, arithmetic and copies ran while one was open for 0% of the time, Pallas kernels for 2%

profile of v5, /device:TPU:1, one launch (start us, length us, event | category | flops | bytes accessed | tf_op | source)
XLA Modules:
  0.0 70.9 jit_solution(16752645617347147355)
XLA Ops:
  0.0 0.0 copy-start
  0.0 5.9 %shard_map.28 = bf16[3072,128]{1,0:T(8,128)(2,1)} custom-call(bf16[3,2048,256]{2,1,0:T(8,128)(2,1)} %volts.1), custom_call_target="tpu_custom_call" | custom-call | flops 3221225472 | bytes 3932160 | tf_op jit(solution)/shard_map/pallas_call | solution.py:166
  5.9 16.5 %all-to-all-start = ((bf16[32,96,128]{2,1,0:T(8,128)(2,1)}), bf16[32,96,128]{2,1,0:T(8,128)(2,1)S(1)}, u32[]{:S(2)}, u32[]{:S(2)}) async-start(bf16[32,96,128]{2,1,0:T(8,128)(2,1)} %bitcast.9), calls=%async_computation | async-start | bytes 1572864 | tf_op jit(solution)/shard_map/all_to_all | solution.py:359
  22.5 23.8 %all-to-all-done = bf16[32,96,128]{2,1,0:T(8,128)(2,1)S(1)} async-done(((bf16[32,96,128]{2,1,0:T(8,128)(2,1)}), bf16[32,96,128]{2,1,0:T(8,128)(2,1)S(1)}, u32[]{:S(2)}, u32[]{:S(2)}) %all-to-all-start) | async-done | bytes 786464 | tf_op jit(solution)/shard_map/all_to_all | solution.py:359
  46.2 0.0 copy-done
  46.2 0.4 shard_map.29
  46.6 15.0 %all_to_all.10 = bf16[8,432,128]{2,1,0:T(8,128)(2,1)S(1)} all-to-all(bf16[8,432,128]{2,1,0:T(8,128)(2,1)S(1)} %bitcast.7), channel_id=1, replica_groups={{0,2,32,34,64,66,96,98},{1,3,33,35,65,67,97,99},{4,6,36,38,68,70,100,10..., dimensions={0} | all-to-all | bytes 1769472 | tf_op jit(solution)/shard_map/all_to_all | solution.py:369
  61.6 0.4 shard_map.30.column
  62.0 5.8 %collective-permute-start = (bf16[1536,256]{1,0:T(8,128)(2,1)S(1)}, bf16[1536,256]{1,0:T(8,128)(2,1)S(1)}, u32[]{:S(2)}, u32[]{:S(2)}) collective-permute-start(bf16[1536,256]{1,0:T(8,128)(2,1)S(1)} %shard_map.30.column), channel_id=1, source_target_pairs={{0,1},{1,0},{2,3},{3,2},{4,5},{5,4},{6,7},{7,6},{8,9},{9,8},{10,11... | collective-permute-start | bytes 2359304 | tf_op jit(solution)/shard_map/ppermute | solution.py:378
  67.8 1.3 %shard_map.31 = (f32[1,256,1024]{2,1,0:T(8,128)}, bf16[2,256,768]{2,1,0:T(8,128)(2,1)S(1)}) custom-call(s32[1]{0:T(128)} %bitcast.place, bf16[1536,256]{1,0:T(8,128)(2,1)S(1)} %shard_map.30.column), custom_call_target="tpu_custom_call" | custom-call | flops 301989888 | bytes 1572864 | tf_op jit(solution)/shard_map/pallas_call | solution.py:389
  69.1 0.6 collective-permute-done.column
  69.7 1.2 %shard_map.32 = f32[1,256,1024]{2,1,0:T(8,128)} custom-call(s32[1]{0:T(128)} %bitcast.place, bf16[2,256,768]{2,1,0:T(8,128)(2,1)S(1)} %get-tuple-element.7.turned, bf16[1536,256]{1,0:T(8,128)(2,1)S(1)} %collective-permute-done.column, f32[1,256,1024]{2,1,0:T(8,128)} %get-tuple-element.8.begun), custom_call_target="tpu_custom_call", output_to_operand_aliasing={{}: (3, {})} | custom-call | flops 301989888 | bytes 1572864 | tf_op jit(solution)/shard_map/pallas_call | solution.py:398
Async XLA Ops:
  0.0 46.2 %copy-start = (f32[128,256]{1,0:T(8,128)S(1)}, f32[128,256]{1,0:T(8,128)}, u32[]{:S(2)}) copy-start(f32[128,256]{1,0:T(8,128)} %gain.1) | copy-start | bytes 393220
  5.9 40.3 %all-to-all-start = ((bf16[32,96,128]{2,1,0:T(8,128)(2,1)}), bf16[32,96,128]{2,1,0:T(8,128)(2,1)S(1)}, u32[]{:S(2)}, u32[]{:S(2)}) async-start(bf16[32,96,128]{2,1,0:T(8,128)(2,1)} %bitcast.9), calls=%async_computation | async-start | bytes 1572864 | tf_op jit(solution)/shard_map/all_to_all | solution.py:359
  62.0 7.7 %collective-permute-start = (bf16[1536,256]{1,0:T(8,128)(2,1)S(1)}, bf16[1536,256]{1,0:T(8,128)(2,1)S(1)}, u32[]{:S(2)}, u32[]{:S(2)}) collective-permute-start(bf16[1536,256]{1,0:T(8,128)(2,1)S(1)} %shard_map.30.column), channel_id=1, source_target_pairs={{0,1},{1,0},{2,3},{3,2},{4,5},{5,4},{6,7},{7,6},{8,9},{9,8},{10,11... | collective-permute-start | bytes 2359304 | tf_op jit(solution)/shard_map/ppermute | solution.py:378

commit v6 on v5

--- a/solution.py
+++ b/solution.py
@@ -242,7 +242,7 @@
     )(place, chunks, channel_gain)
 
 
-def column_kernel(count, sources, pieces, column, carried):
+def build_column(count, sources, pieces, column, carried, chip):
     width = column.shape[1]
     halves = width // LANES
     half = count * 2 * halves
@@ -250,48 +250,34 @@
     length = half * (sources + runs)
     steps = LONG * sources
     first_of_run = lax.broadcasted_iota(jnp.int32, (LONG * runs, DEEP, LANES), 1) == 0
-    for chip in range(2):
-        carried[:half, :] = jnp.zeros((half, LANES), jnp.float32)
-        for x in range(LONG):
-            at = (x * 2 + chip) * length + half * sources
-            ends = pieces[at : at + half * runs, :].astype(jnp.float32)
-            for y in range(runs):
-                run = y * LONG + x + 1
-                if run < LONG * runs:
-                    to = (run % LONG * runs + run // LONG) * half
-                    carried[to : to + half, :] = ends[y * half : (y + 1) * half]
-        for r in range(half):
-            sp, h = r // halves, r % halves
-            own = jnp.concatenate(
-                [
-                    pieces[
-                        (x * 2 + chip) * length + r * sources : (x * 2 + chip) * length
-                        + (r + 1) * sources,
-                        :,
-                    ]
-                    for x in range(LONG)
-                ],
-                0,
-            ).astype(jnp.float32)
-            begun = carried[pl.ds(r, LONG * runs, stride=half), :]
-            begun = jnp.where(first_of_run, begun[:, None, :], 0.0).reshape(steps, LANES)
-            at = (chip * count * 2 + sp) * steps
-            column[at : at + steps, h * LANES : (h + 1) * LANES] = (own + begun).astype(
-                jnp.bfloat16
-            )
-
-
-def both_columns(pieces, count, width, groups):
-    half = count * 2 * (width // LANES)
-    sources = groups // LONG
-    return pl.pallas_call(
-        functools.partial(column_kernel, count, sources),
-        out_shape=jax.ShapeDtypeStruct((4 * count * groups, width), jnp.bfloat16),
-        in_specs=[pl.BlockSpec(memory_space=pltpu.VMEM)],
-        out_specs=pl.BlockSpec(memory_space=pltpu.VMEM),
-        scratch_shapes=[pltpu.VMEM((half * (groups // DEEP + 1), LANES), jnp.float32)],
-        compiler_params=pltpu.CompilerParams(vmem_limit_bytes=16 * 1024 * 1024),
-    )(pieces)
+    carried[:half, :] = jnp.zeros((half, LANES), jnp.float32)
+    for x in range(LONG):
+        at = (x * 2 + chip) * length + half * sources
+        ends = pieces[at : at + half * runs, :].astype(jnp.float32)
+        for y in range(runs):
+            run = y * LONG + x + 1
+            if run < LONG * runs:
+                to = (run % LONG * runs + run // LONG) * half
+                carried[to : to + half, :] = ends[y * half : (y + 1) * half]
+    for r in range(half):
+        sp, h = r // halves, r % halves
+        own = jnp.concatenate(
+            [
+                pieces[
+                    (x * 2 + chip) * length + r * sources : (x * 2 + chip) * length
+                    + (r + 1) * sources,
+                    :,
+                ]
+                for x in range(LONG)
+            ],
+            0,
+        ).astype(jnp.float32)
+        begun = carried[pl.ds(r, LONG * runs, stride=half), :]
+        begun = jnp.where(first_of_run, begun[:, None, :], 0.0).reshape(steps, LANES)
+        at = (chip * count * 2 + sp) * steps
+        column[at : at + steps, h * LANES : (h + 1) * LANES] = (own + begun).astype(
+            jnp.bfloat16
+        )
 
 
 def product(left, right):
@@ -309,10 +295,12 @@
         copy.wait()
 
 
-def near_kernel(groups, norm_scale, place, column, out, turned, block, sems):
+def near_kernel(count, groups, norm_scale, place, pieces, out, turned, column, carried, block, sems):
     rows, width = column.shape[0] // 2, column.shape[1]
     mine = place[0]
     chip = mine // 2
+    for which in range(2):
+        build_column(count, groups // LONG, pieces, column, carried, which)
     own = column[pl.ds(pl.multiple_of(chip * rows, rows), rows), :]
     far = column[pl.ds(pl.multiple_of((1 - chip) * rows, rows), rows), :]
     turned[0] = own.T
@@ -331,15 +319,20 @@
     place_blocks(width, parts, out, block, sems)
 
 
-def last_kernel(norm_scale, place, turned, column, begun, out, block, sems):
+def last_kernel(count, groups, norm_scale, place, turned, pieces, begun, out, column, carried, block, sems):
     rows, width = column.shape[0] // 2, column.shape[1]
     mine = place[0]
-    parts = []
+    copies = []
     for chip in range(2):
+        build_column(count, groups // LONG, pieces, column, carried, chip)
         other = (mine ^ 1) % 2 + 2 * chip
         left = turned[(other < mine).astype(jnp.int32)]
-        parts.append((other, product(left, column[chip * rows : (chip + 1) * rows]) * norm_scale))
-    place_blocks(width, parts, out, block, sems)
+        block[chip] = product(left, column[chip * rows : (chip + 1) * rows]) * norm_scale
+        columns = pl.ds(pl.multiple_of(other * width, width), width)
+        copies.append(pltpu.make_async_copy(block.at[chip], out.at[0, :, columns], sems.at[chip]))
+        copies[-1].start()
+    for copy in copies:
+        copy.wait()
 
 
 def shards(voltages, channel_gain):
@@ -374,29 +367,35 @@
         tiled=True,
         axis_index_groups=same_yz,
     )
-    column = both_columns(spread.reshape(-1, LANES), count, width, groups)
-    other_column = lax.ppermute(column, "inp", [(i, i ^ 1) for i in range(4)])
-    rows = column.shape[0] // 2
+    pieces = spread.reshape(-1, LANES)
+    other_pieces = lax.ppermute(pieces, "inp", [(i, i ^ 1) for i in range(4)])
+    rows = 2 * count * groups
     in_smem = pl.BlockSpec(memory_space=pltpu.SMEM)
     in_vmem = pl.BlockSpec(memory_space=pltpu.VMEM)
     anywhere = pl.BlockSpec(memory_space=pl.ANY)
     shape = jax.ShapeDtypeStruct((1, width, 4 * width), jnp.float32)
-    scratch = [pltpu.VMEM((2, width, width), jnp.float32), pltpu.SemaphoreType.DMA((2,))]
+    half = count * 2 * (width // LANES)
+    scratch = [
+        pltpu.VMEM((2 * rows, width), jnp.bfloat16),
+        pltpu.VMEM((half * (groups // DEEP + 1), LANES), jnp.float32),
+        pltpu.VMEM((2, width, width), jnp.float32),
+        pltpu.SemaphoreType.DMA((2,)),
+    ]
     limits = pltpu.CompilerParams(vmem_limit_bytes=16 * 1024 * 1024)
     cost = pl.CostEstimate(
         flops=6 * rows * width * width, bytes_accessed=8 * rows * width, transcendentals=0
     )
     begun, left = pl.pallas_call(
-        functools.partial(near_kernel, groups, norm_scale),
+        functools.partial(near_kernel, count, groups, norm_scale),
         out_shape=(shape, jax.ShapeDtypeStruct((2, width, rows), jnp.bfloat16)),
         in_specs=[in_smem, in_vmem],
         out_specs=(anywhere, in_vmem),
         scratch_shapes=scratch,
         compiler_params=limits,
         cost_estimate=cost,
-    )(place, column)
+    )(place, pieces)
     return pl.pallas_call(
-        functools.partial(last_kernel, norm_scale),
+        functools.partial(last_kernel, count, groups, norm_scale),
         out_shape=shape,
         in_specs=[in_smem, in_vmem, in_vmem, anywhere],
         out_specs=anywhere,
@@ -404,7 +403,7 @@
         input_output_aliases={3: 0},
         compiler_params=limits,
         cost_estimate=cost,
-    )(place, left, other_column, begun)
+    )(place, left, other_pieces, begun)
 
 
 def solution(mesh):

time: 71.2 us -> 71.2 us (level)
    pallas_call x3 -> x2, Pallas kernels: 2.87 us -> 3.17 us  [the longest x1 1.68 us: shards(): pl.pallas_call(functools.partial(near_kernel, count, groups, norm_scale),...]
where the time goes in v6:
time: 71.2 us; the launch traced here: 70.9 us
  waiting for transfers between devices  24.1 us (34%)
  starting transfers between devices  22.3 us (31%)
  blocking collectives  15 us (21%)
  Pallas kernels  9.44 us (13%)
    all_to_all x1, waiting for transfers between devices, shards(): lax.all_to_all(chunks, 'tf', split_axis=0, concat_axis=0, tiled=True, axi...  23.8 us
    all_to_all x1, starting transfers between devices, shards(): lax.all_to_all(chunks, 'tf', split_axis=0, concat_axis=0, tiled=True, axi...  16.5 us
    all_to_all x1, blocking collectives, shards(): lax.all_to_all(pieces.reshape(2 * LONG, -1, LANES), ('tf', 'inp'), split_...  15 us
    pallas_call x1, Pallas kernels, partial_spectra(): pl.pallas_call(partial_kernel, out_shape=jax.ShapeDtypeStruct((channels *...  5.89 us
    ppermute x1, starting transfers between devices, shards(): other_pieces = lax.ppermute(pieces, 'inp', [(i, i ^ 1) for i in range(4)])  5.76 us
    pallas_call x1, Pallas kernels, shards(): pl.pallas_call(functools.partial(near_kernel, count, groups, norm_scale),...  1.68 us
    pallas_call x1, Pallas kernels, shards(): pl.pallas_call(functools.partial(last_kernel, count, groups, norm_scale),...  1.48 us
  transfers between devices with their start and end apart: 2, of which 2 were waited for; matrix products, arithmetic and copies ran while one was open for 0% of the time, Pallas kernels for 2%

profile of v6, /device:TPU:1, one launch (start us, length us, event | category | flops | bytes accessed | tf_op | source)
XLA Modules:
  0.0 70.9 jit_solution(11299520498904328583)
XLA Ops:
  0.0 0.0 copy-start
  0.0 5.9 %shard_map.28 = bf16[3072,128]{1,0:T(8,128)(2,1)} custom-call(bf16[3,2048,256]{2,1,0:T(8,128)(2,1)} %volts.1), custom_call_target="tpu_custom_call" | custom-call | flops 3221225472 | bytes 3932160 | tf_op jit(solution)/shard_map/pallas_call | solution.py:166
  5.9 16.5 %all-to-all-start = ((bf16[32,96,128]{2,1,0:T(8,128)(2,1)}), bf16[32,96,128]{2,1,0:T(8,128)(2,1)S(1)}, u32[]{:S(2)}, u32[]{:S(2)}) async-start(bf16[32,96,128]{2,1,0:T(8,128)(2,1)} %bitcast.10), calls=%async_computation | async-start | bytes 1572864 | tf_op jit(solution)/shard_map/all_to_all | solution.py:352
  22.5 23.8 %all-to-all-done = bf16[32,96,128]{2,1,0:T(8,128)(2,1)S(1)} async-done(((bf16[32,96,128]{2,1,0:T(8,128)(2,1)}), bf16[32,96,128]{2,1,0:T(8,128)(2,1)S(1)}, u32[]{:S(2)}, u32[]{:S(2)}) %all-to-all-start) | async-done | bytes 786464 | tf_op jit(solution)/shard_map/all_to_all | solution.py:352
  46.2 0.0 copy-done
  46.2 0.4 shard_map.29
  46.6 15.0 %all_to_all.10 = bf16[8,432,128]{2,1,0:T(8,128)(2,1)S(1)} all-to-all(bf16[8,432,128]{2,1,0:T(8,128)(2,1)S(1)} %bitcast.6), channel_id=1, replica_groups={{0,2,32,34,64,66,96,98},{1,3,33,35,65,67,97,99},{4,6,36,38,68,70,100,10..., dimensions={0} | all-to-all | bytes 1769472 | tf_op jit(solution)/shard_map/all_to_all | solution.py:362
  61.6 5.8 %collective-permute-start = (bf16[3456,128]{1,0:T(8,128)(2,1)S(1)}, bf16[3456,128]{1,0:T(8,128)(2,1)S(1)}, u32[]{:S(2)}, u32[]{:S(2)}) collective-permute-start(bf16[3456,128]{1,0:T(8,128)(2,1)S(1)} %bitcast.8), channel_id=1, source_target_pairs={{0,1},{1,0},{2,3},{3,2},{4,5},{5,4},{6,7},{7,6},{8,9},{9,8},{10,11... | collective-permute-start | bytes 2654216 | tf_op jit(solution)/shard_map/ppermute | solution.py:371
  67.4 1.7 %shard_map.30 = (f32[1,256,1024]{2,1,0:T(8,128)}, bf16[2,256,768]{2,1,0:T(8,128)(2,1)S(1)}) custom-call(s32[1]{0:T(128)} %bitcast.place, bf16[3456,128]{1,0:T(8,128)(2,1)S(1)} %bitcast.9), custom_call_target="tpu_custom_call" | custom-call | flops 301989888 | bytes 1572864 | tf_op jit(solution)/shard_map/pallas_call | solution.py:388
  69.1 0.3 collective-permute-done.pieces
  69.4 1.5 %shard_map.31 = f32[1,256,1024]{2,1,0:T(8,128)} custom-call(s32[1]{0:T(128)} %bitcast.place, bf16[2,256,768]{2,1,0:T(8,128)(2,1)S(1)} %get-tuple-element.7.turned, bf16[3456,128]{1,0:T(8,128)(2,1)S(1)} %collective-permute-done.pieces, f32[1,256,1024]{2,1,0:T(8,128)} %get-tuple-element.8.begun), custom_call_target="tpu_custom_call", output_to_operand_aliasing={{}: (3, {})} | custom-call | flops 301989888 | bytes 1572864 | tf_op jit(solution)/shard_map/pallas_call | solution.py:397
Async XLA Ops:
  0.0 46.2 %copy-start = (f32[128,256]{1,0:T(8,128)S(1)}, f32[128,256]{1,0:T(8,128)}, u32[]{:S(2)}) copy-start(f32[128,256]{1,0:T(8,128)} %gain.1) | copy-start | bytes 393220
  5.9 40.3 %all-to-all-start = ((bf16[32,96,128]{2,1,0:T(8,128)(2,1)}), bf16[32,96,128]{2,1,0:T(8,128)(2,1)S(1)}, u32[]{:S(2)}, u32[]{:S(2)}) async-start(bf16[32,96,128]{2,1,0:T(8,128)(2,1)} %bitcast.10), calls=%async_computation | async-start | bytes 1572864 | tf_op jit(solution)/shard_map/all_to_all | solution.py:352
  61.6 7.8 %collective-permute-start = (bf16[3456,128]{1,0:T(8,128)(2,1)S(1)}, bf16[3456,128]{1,0:T(8,128)(2,1)S(1)}, u32[]{:S(2)}, u32[]{:S(2)}) collective-permute-start(bf16[3456,128]{1,0:T(8,128)(2,1)S(1)} %bitcast.8), channel_id=1, source_target_pairs={{0,1},{1,0},{2,3},{3,2},{4,5},{5,4},{6,7},{7,6},{8,9},{9,8},{10,11... | collective-permute-start | bytes 2654216 | tf_op jit(solution)/shard_map/ppermute | solution.py:371

commit v7 on v5

--- a/solution.py
+++ b/solution.py
@@ -131,7 +131,7 @@
         store(s, meet(max(1, s + 1 - TAPS), min(count, s + 1), s), s < TAPS)
 
     size = touched * 2 * halves
-    together = 2
+    together = LONG
     blocks = 4
     steps = channels // together // blocks
 
@@ -150,7 +150,7 @@
 
     out_copies = []
     for block in range(blocks):
-        lax.fori_loop(block * steps, (block + 1) * steps, turn, 0, unroll=16)
+        lax.fori_loop(block * steps, (block + 1) * steps, turn, 0, unroll=8)
         part = pl.ds(block * steps * together * size, steps * together * size)
         out_copies.append(
             pltpu.make_async_copy(turned.at[part], chunks.at[part], out_sems.at[block])

time: 71.2 us -> 71.2 us (level)
  no operation moved by 1% of the time
where the time goes in v7:
time: 71.2 us; the launch traced here: 70.9 us
  waiting for transfers between devices  24.3 us (34%)
  starting transfers between devices  22.3 us (31%)
  blocking collectives  15 us (21%)
  Pallas kernels  9.14 us (13%)
    all_to_all x1, waiting for transfers between devices, shards(): lax.all_to_all(chunks, 'tf', split_axis=0, concat_axis=0, tiled=True, axi...  23.8 us
    all_to_all x1, starting transfers between devices, shards(): lax.all_to_all(chunks, 'tf', split_axis=0, concat_axis=0, tiled=True, axi...  16.5 us
    all_to_all x1, blocking collectives, shards(): lax.all_to_all(pieces.reshape(2 * LONG, -1, LANES), ('tf', 'inp'), split_...  15 us
    pallas_call x1, Pallas kernels, partial_spectra(): pl.pallas_call(partial_kernel, out_shape=jax.ShapeDtypeStruct((channels *...  5.89 us
    ppermute x1, starting transfers between devices, shards(): other_column = lax.ppermute(column, 'inp', [(i, i ^ 1) for i in range(4)])  5.77 us
  transfers between devices with their start and end apart: 2, of which 2 were waited for; matrix products, arithmetic and copies ran while one was open for 0% of the time, Pallas kernels for 2%

profile of v7, /device:TPU:1, one launch (start us, length us, event | category | flops | bytes accessed | tf_op | source)
XLA Modules:
  0.0 70.9 jit_solution(16752645617347147355)
XLA Ops:
  0.0 0.0 copy-start
  0.0 5.9 %shard_map.28 = bf16[3072,128]{1,0:T(8,128)(2,1)} custom-call(bf16[3,2048,256]{2,1,0:T(8,128)(2,1)} %volts.1), custom_call_target="tpu_custom_call" | custom-call | flops 3221225472 | bytes 3932160 | tf_op jit(solution)/shard_map/pallas_call | solution.py:166
  5.9 16.5 %all-to-all-start = ((bf16[32,96,128]{2,1,0:T(8,128)(2,1)}), bf16[32,96,128]{2,1,0:T(8,128)(2,1)S(1)}, u32[]{:S(2)}, u32[]{:S(2)}) async-start(bf16[32,96,128]{2,1,0:T(8,128)(2,1)} %bitcast.9), calls=%async_computation | async-start | bytes 1572864 | tf_op jit(solution)/shard_map/all_to_all | solution.py:359
  22.5 23.8 %all-to-all-done = bf16[32,96,128]{2,1,0:T(8,128)(2,1)S(1)} async-done(((bf16[32,96,128]{2,1,0:T(8,128)(2,1)}), bf16[32,96,128]{2,1,0:T(8,128)(2,1)S(1)}, u32[]{:S(2)}, u32[]{:S(2)}) %all-to-all-start) | async-done | bytes 786464 | tf_op jit(solution)/shard_map/all_to_all | solution.py:359
  46.2 0.0 copy-done
  46.2 0.4 shard_map.29
  46.6 15.0 %all_to_all.10 = bf16[8,432,128]{2,1,0:T(8,128)(2,1)S(1)} all-to-all(bf16[8,432,128]{2,1,0:T(8,128)(2,1)S(1)} %bitcast.7), channel_id=1, replica_groups={{0,2,32,34,64,66,96,98},{1,3,33,35,65,67,97,99},{4,6,36,38,68,70,100,10..., dimensions={0} | all-to-all | bytes 1769472 | tf_op jit(solution)/shard_map/all_to_all | solution.py:369
  61.6 0.4 shard_map.30.column
  62.0 5.8 %collective-permute-start = (bf16[1536,256]{1,0:T(8,128)(2,1)S(1)}, bf16[1536,256]{1,0:T(8,128)(2,1)S(1)}, u32[]{:S(2)}, u32[]{:S(2)}) collective-permute-start(bf16[1536,256]{1,0:T(8,128)(2,1)S(1)} %shard_map.30.column), channel_id=1, source_target_pairs={{0,1},{1,0},{2,3},{3,2},{4,5},{5,4},{6,7},{7,6},{8,9},{9,8},{10,11... | collective-permute-start | bytes 2359304 | tf_op jit(solution)/shard_map/ppermute | solution.py:378
  67.8 1.3 %shard_map.31 = (f32[1,256,1024]{2,1,0:T(8,128)}, bf16[2,256,768]{2,1,0:T(8,128)(2,1)S(1)}) custom-call(s32[1]{0:T(128)} %bitcast.place, bf16[1536,256]{1,0:T(8,128)(2,1)S(1)} %shard_map.30.column), custom_call_target="tpu_custom_call" | custom-call | flops 301989888 | bytes 1572864 | tf_op jit(solution)/shard_map/pallas_call | solution.py:389
  69.1 0.6 collective-permute-done.column
  69.7 1.2 %shard_map.32 = f32[1,256,1024]{2,1,0:T(8,128)} custom-call(s32[1]{0:T(128)} %bitcast.place, bf16[2,256,768]{2,1,0:T(8,128)(2,1)S(1)} %get-tuple-element.7.turned, bf16[1536,256]{1,0:T(8,128)(2,1)S(1)} %collective-permute-done.column, f32[1,256,1024]{2,1,0:T(8,128)} %get-tuple-element.8.begun), custom_call_target="tpu_custom_call", output_to_operand_aliasing={{}: (3, {})} | custom-call | flops 301989888 | bytes 1572864 | tf_op jit(solution)/shard_map/pallas_call | solution.py:398
Async XLA Ops:
  0.0 46.2 %copy-start = (f32[128,256]{1,0:T(8,128)S(1)}, f32[128,256]{1,0:T(8,128)}, u32[]{:S(2)}) copy-start(f32[128,256]{1,0:T(8,128)} %gain.1) | copy-start | bytes 393220
  5.9 40.3 %all-to-all-start = ((bf16[32,96,128]{2,1,0:T(8,128)(2,1)}), bf16[32,96,128]{2,1,0:T(8,128)(2,1)S(1)}, u32[]{:S(2)}, u32[]{:S(2)}) async-start(bf16[32,96,128]{2,1,0:T(8,128)(2,1)} %bitcast.9), calls=%async_computation | async-start | bytes 1572864 | tf_op jit(solution)/shard_map/all_to_all | solution.py:359
  62.0 7.7 %collective-permute-start = (bf16[1536,256]{1,0:T(8,128)(2,1)S(1)}, bf16[1536,256]{1,0:T(8,128)(2,1)S(1)}, u32[]{:S(2)}, u32[]{:S(2)}) collective-permute-start(bf16[1536,256]{1,0:T(8,128)(2,1)S(1)} %shard_map.30.column), channel_id=1, source_target_pairs={{0,1},{1,0},{2,3},{3,2},{4,5},{5,4},{6,7},{7,6},{8,9},{9,8},{10,11... | collective-permute-start | bytes 2359304 | tf_op jit(solution)/shard_map/ppermute | solution.py:378
